TPU v7x, 512 devices: a whole 4x8x8 slice. The times are simulated.
512 devices in a mesh: lon: 32 (over y_lo, z, core), lat: 16 (over y_hi, x).
Axes of the slice: x: 4, y: 8 (y_hi: 4, y_lo: 2; y = y_hi * 2 + y_lo), z: 8, core: 2. Of those that a mesh axis runs over, the one named last changes fastest.
Arguments:
- queries: bfloat16 [256, 256, 1024], P('lat', 'lon'), may hold values from -6 to 6
- keys: bfloat16 [256, 256, 1024], P('lat', 'lon'), may hold values from -6 to 6
- values: bfloat16 [256, 256, 1024], P('lat', 'lon'), may hold values from -6 to 6
- cotangent: bfloat16 [256, 256, 1024], P('lat', 'lon'), may hold values from -6 to 6
Outputs:
- attended: bfloat16 [256, 256, 1024], P('lat', 'lon')
- grad_queries: bfloat16 [256, 256, 1024], P('lat', 'lon')
- grad_keys: bfloat16 [256, 256, 1024], P('lat', 'lon')
- grad_values: bfloat16 [256, 256, 1024], P('lat', 'lon')
All inputs are finite; a program needn't handle non-finite values.
Results may differ from a plain program's by a relative error of at most 0.0076.
Values may be sent and summed in bfloat16 or wider, within the bound.
A program may use at most 64 MiB of HBM per device.

v0:
```python
import jax
import jax.numpy as jnp
from jax import lax
from jax.sharding import PartitionSpec as P

HEADS = 16
RADIUS = 6


def extended_2(value, sides, width):
    for axis, dim in sides:
        peers, length = (lax.axis_size(axis), value.shape[dim])
        up = [(i, (i + 1) % peers) for i in range(peers)]
        down = [(j, i) for i, j in up]
        last = lax.slice_in_dim(value, length - width, length, axis=dim)
        leading = lax.slice_in_dim(value, 0, width, axis=dim)
        before = lax.ppermute(last, axis, up)
        after = lax.ppermute(leading, axis, down)
        value = jnp.concatenate([before, value, after], axis=dim)
    return value


def passed_along(block, axis, distance):
    devices = range(lax.axis_size(axis))
    route = [(i - distance, i) for i in devices if i - distance in devices]
    return lax.ppermute(block, axis, route)


def from_behind(value, axis, by):
    peers = lax.axis_size(axis)
    return lax.ppermute(value, axis, [(i, (i + by) % peers) for i in range(peers)])


def window_mask(query_row, query_col, key_row, key_col, total_rows):
    start = jnp.clip(query_row - RADIUS, 0, total_rows - 2 * RADIUS - 1)
    inside = (key_row[None, :] >= start[:, None]) & (
        key_row[None, :] <= start[:, None] + 2 * RADIUS
    )
    near = jnp.abs(key_col[None, :] - query_col[:, None]) <= RADIUS
    valid = (query_row >= 0) & (query_row < total_rows)
    return inside & near & valid[:, None]


def to_groups(field, groups):
    tokens = field.shape[0] * field.shape[1]
    head_dim = field.shape[2] // HEADS
    return field.reshape(tokens, groups, HEADS // groups, head_dim).transpose(1, 0, 2, 3)


def from_groups(field, rows_out, cols_out):
    return field.transpose(1, 0, 2, 3).reshape(rows_out, cols_out, -1)


def attend(query_blk, key_blk, value_blk, cot_blk, mask, scale):
    scores = (
        jnp.einsum("nhd,ehd->hne", query_blk, key_blk, preferred_element_type=jnp.float32) * scale
    )
    scores = jnp.where(mask[None], scores, -jnp.inf)
    highest = jnp.max(scores, axis=2, keepdims=True)
    log_norm = highest + jnp.log(jnp.sum(jnp.exp(scores - highest), axis=2, keepdims=True))
    weights = jnp.exp(scores - log_norm)
    rounded = weights.astype(jnp.bfloat16)
    attended = jnp.einsum(
        "hne,ehd->nhd", rounded, value_blk, preferred_element_type=jnp.float32
    ).astype(jnp.bfloat16)
    weight_grads = jnp.einsum(
        "nhd,ehd->hne", cot_blk, value_blk, preferred_element_type=jnp.float32
    )
    delta = jnp.sum(weights * weight_grads, axis=2, keepdims=True)
    score_grads = (weights * (weight_grads - delta)).astype(jnp.bfloat16)
    grad_query = (
        jnp.einsum("hne,ehd->nhd", score_grads, key_blk, preferred_element_type=jnp.float32) * scale
    ).astype(jnp.bfloat16)
    return (attended, grad_query, log_norm[:, :, 0], delta[:, :, 0], score_grads, rounded)


def shards(queries, keys, values, cotangent):
    rows_dev, cols_dev, width = queries.shape
    head_dim = width // HEADS
    scale = head_dim ** (-0.5)
    groups = HEADS // 4
    ext_rows = rows_dev + 2 * RADIUS
    ext_cols = cols_dev + 2 * RADIUS
    total_rows = rows_dev * lax.axis_size("lat")
    first_row = lax.axis_index("lat") * rows_dev
    paired = jnp.concatenate([keys, values], axis=2)
    extended = extended_2(paired, (("lon", 1), ("lat", 0)), RADIUS)
    key_ext = to_groups(extended[:, :, :width], groups)
    value_ext = to_groups(extended[:, :, width:], groups)
    own_rows = first_row + jnp.repeat(jnp.arange(rows_dev, dtype=jnp.int32), cols_dev)
    own_cols = jnp.tile(jnp.arange(cols_dev, dtype=jnp.int32), rows_dev) + RADIUS
    rim_rows = first_row - RADIUS + jnp.repeat(jnp.arange(ext_rows, dtype=jnp.int32), ext_cols)
    rim_cols = jnp.tile(jnp.arange(ext_cols, dtype=jnp.int32), ext_rows)
    query_mask = window_mask(own_rows, own_cols, rim_rows, rim_cols, total_rows)
    query_groups = to_groups(queries, groups)
    cot_groups = to_groups(cotangent, groups)
    inputs = (query_groups, key_ext, value_ext, cot_groups)

    def with_partials(items):
        attended, grad_query, log_norm, delta, score_grads, rounded = attend(
            *items, query_mask, scale
        )
        grad_key = (
            jnp.einsum("hne,nhd->ehd", score_grads, items[0], preferred_element_type=jnp.float32)
            * scale
        )
        grad_value = jnp.einsum(
            "hne,nhd->ehd", rounded, items[3], preferred_element_type=jnp.float32
        )
        return (attended, grad_query, grad_key, grad_value)

    out_groups, dq_groups, dk_groups, dv_groups = lax.map(with_partials, inputs)
    partial_value = jnp.concatenate(
        [from_groups(dk_groups, ext_rows, ext_cols), from_groups(dv_groups, ext_rows, ext_cols)],
        axis=2,
    )
    upper_rim = partial_value[:RADIUS]
    lower_rim = partial_value[rows_dev + RADIUS :]
    from_next = passed_along(upper_rim, "lat", -1)
    from_prev = passed_along(lower_rim, "lat", 1)
    middle = partial_value[RADIUS : rows_dev + RADIUS]
    middle = middle.at[:RADIUS].add(from_prev)
    middle = middle.at[rows_dev - RADIUS :].add(from_next)
    west_rim = middle[:, :RADIUS]
    east_rim = middle[:, cols_dev + RADIUS :]
    from_east = from_behind(west_rim, "lon", -1)
    from_west = from_behind(east_rim, "lon", 1)
    folded = middle[:, RADIUS : cols_dev + RADIUS]
    folded = folded.at[:, :RADIUS].add(from_west)
    folded = folded.at[:, cols_dev - RADIUS :].add(from_east)
    grad_keys = folded[:, :, :width].astype(jnp.bfloat16)
    grad_values = folded[:, :, width:].astype(jnp.bfloat16)
    attended = from_groups(out_groups, rows_dev, cols_dev)
    grad_queries = from_groups(dq_groups, rows_dev, cols_dev)
    return (attended, grad_queries, grad_keys, grad_values)


def solution(mesh):
    placed = (
        P("lat", "lon", None),
        P("lat", "lon", None),
        P("lat", "lon", None),
        P("lat", "lon", None),
    )
    return jax.shard_map(
        shards,
        mesh=mesh,
        in_specs=placed,
        out_specs=(
            P("lat", "lon", None),
            P("lat", "lon", None),
            P("lat", "lon", None),
            P("lat", "lon", None),
        ),
        check_vma=False,
    )
```

profile of v0, /device:TPU:22, one launch (start us, length us, event | category | flops | bytes accessed | tf_op | source)
XLA Modules:
  0.0 216.0 jit_solution(12999717718920132130)
XLA Ops:
  0.6 1.0 constant_dynamic-update-slice_fusion.1
  1.6 1.0 constant_dynamic-update-slice_fusion
  2.7 1.9 collective-permute-start
  4.7 11.4 %collective-permute-start.1 = (bf16[16,6,2048]{2,1,0:T(8,128)(2,1)S(1)}, bf16[16,6,2048]{2,1,0:T(8,128)(2,1)S(1)}, u32[]{:S(2)}, u32[]{:S(2)}) collective-permute-start(bf16[16,6,2048]{2,1,0:T(8,128)(2,1)S(1)} %get-tuple-element.224), channel_id=1, source_target_pairs={{16,0},{32,16},{48,32},{64,48},{80,64},{96,80},{112,96},{128,112},... | collective-permute-start | bytes 1179656 | tf_op jit(solution)/shard_map/ppermute | solution.py:18
  16.1 4.9 %collective-permute-done = bf16[16,6,2048]{2,1,0:T(8,128)(2,1)S(1)} collective-permute-done((bf16[16,6,2048]{2,1,0:T(8,128)(2,1)S(1)}, bf16[16,6,2048]{2,1,0:T(8,128)(2,1)S(1)}, u32[]{:S(2)}, u32[]{:S(2)}) %collective-permute-start) | collective-permute-done | bytes 393248 | tf_op jit(solution)/shard_map/ppermute | solution.py:17
  21.0 1.8 collective-permute-done.1
  22.7 1.5 pad_maximum_fusion.3
  24.2 4.8 %collective-permute-start.2 = (bf16[6,20,2048]{2,1,0:T(8,128)(2,1)}, bf16[6,20,2048]{2,1,0:T(8,128)(2,1)S(1)}, u32[]{:S(2)}, u32[]{:S(2)}) collective-permute-start(bf16[6,20,2048]{2,1,0:T(8,128)(2,1)} %get-tuple-element.219), channel_id=1, source_target_pairs={{0,1},{1,2},{2,3},{3,4},{4,5},{5,6},{6,7},{7,8},{8,9},{9,10},{10,1... | collective-permute-start | bytes 1474568 | tf_op jit(solution)/shard_map/ppermute | solution.py:17
  29.1 1.9 collective-permute-start.3
  33.2 17.6 %collective-permute-done.2 = bf16[6,20,2048]{2,1,0:T(8,128)(2,1)S(1)} collective-permute-done((bf16[6,20,2048]{2,1,0:T(8,128)(2,1)}, bf16[6,20,2048]{2,1,0:T(8,128)(2,1)S(1)}, u32[]{:S(2)}, u32[]{:S(2)}) %collective-permute-start.2) | collective-permute-done | bytes 491552 | tf_op jit(solution)/shard_map/ppermute | solution.py:17
  50.8 7.6 %collective-permute-done.3 = bf16[6,20,2048]{2,1,0:T(8,128)(2,1)} collective-permute-done((bf16[6,20,2048]{2,1,0:T(8,128)(2,1)}, bf16[6,20,2048]{2,1,0:T(8,128)(2,1)}, u32[]{:S(2)}, u32[]{:S(2)}) %collective-permute-start.3) | collective-permute-done | bytes 491552 | tf_op jit(solution)/shard_map/ppermute | solution.py:18
  58.4 2.0 pad_maximum_fusion
  60.4 1.4 fusion.47
  61.8 5.4 %reshape.209 = bf16[560,4,4,64]{3,2,1,0:T(4,128)(2,1)} reshape(bf16[28,20,1024]{2,1,0:T(8,128)(2,1)} %get-tuple-element.217) | data formatting | bytes 2293760 | tf_op jit(solution)/shard_map/reshape | solution.py:47
  67.1 3.1 %copy.26 = bf16[4,560,4,64]{1,3,2,0:T(8,128)(2,1)S(1)} copy(bf16[4,560,4,64]{3,2,0,1:T(4,128)(2,1)} %bitcast.90) | data formatting | bytes 2293760
  70.3 2.6 %reshape.207 = bf16[560,4,4,64]{3,2,1,0:T(4,128)(2,1)} reshape(bf16[28,20,1024]{2,1,0:T(8,128)(2,1)S(1)} %get-tuple-element.218) | data formatting | bytes 2293760 | tf_op jit(solution)/shard_map/reshape | solution.py:47
  72.9 3.1 %copy.24 = bf16[4,560,4,64]{1,3,2,0:T(8,128)(2,1)S(1)} copy(bf16[4,560,4,64]{3,2,0,1:T(4,128)(2,1)} %bitcast.91) | data formatting | bytes 2293760
  76.0 20.5 %while.21 = (s32[]{:T(128)}, bf16[4,128,4,64]{1,3,2,0:T(8,128)(2,1)}, bf16[4,128,4,64]{1,3,2,0:T(8,128)(2,1)S(1)}, f32[4,560,4,64]{1,3,2,0:T(8,128)}, f32[4,560,...) while((s32[]{:T(128)}, ...), condition=%wide.region_4.5_spmd.clone, body=%wide.region_0.4_spmd.clone.sunk | while | flops 225602560 | bytes 14090397 | solution.py:112
  78.7 1.2 fusion.79
  79.9 1.2 fusion.78
  83.8 1.3 fusion.79
  85.1 1.2 fusion.78
  89.0 1.3 fusion.79
  90.3 1.2 fusion.78
  94.2 1.2 fusion.79
  95.3 1.2 fusion.78
  96.5 5.1 %copy.31 = f32[560,4,4,64]{3,2,1,0:T(4,128)} copy(f32[560,4,4,64]{0,3,2,1:T(8,128)} %bitcast.92) | data formatting | bytes 4587520 | tf_op jit(solution)/shard_map/transpose | solution.py:51
  101.6 4.9 %reshape.214 = f32[28,20,1024]{2,1,0:T(8,128)S(1)} reshape(f32[560,4,4,64]{3,2,1,0:T(4,128)} %copy.31) | data formatting | bytes 4587520 | tf_op jit(solution)/shard_map/reshape | solution.py:51
  106.5 5.1 %copy.30 = f32[560,4,4,64]{3,2,1,0:T(4,128)} copy(f32[560,4,4,64]{0,3,2,1:T(8,128)} %bitcast.93) | data formatting | bytes 4587520 | tf_op jit(solution)/shard_map/transpose | solution.py:51
  111.6 5.9 %reshape.213 = f32[28,20,1024]{2,1,0:T(8,128)} reshape(f32[560,4,4,64]{3,2,1,0:T(4,128)} %copy.30) | data formatting | bytes 4587520 | tf_op jit(solution)/shard_map/reshape | solution.py:51
  117.5 2.0 constant_dynamic-update-slice_fusion.3
  120.0 1.9 collective-permute-start.4
  121.9 4.1 %collective-permute-start.5 = (f32[6,20,2048]{2,1,0:T(8,128)S(1)}, f32[6,20,2048]{2,1,0:T(8,128)S(1)}, u32[]{:S(2)}, u32[]{:S(2)}) collective-permute-start(f32[6,20,2048]{2,1,0:T(8,128)S(1)} %get-tuple-element.213), channel_id=1, source_target_pairs={{1,0},{2,1},{3,2},{4,3},{5,4},{6,5},{7,6},{8,7},{9,8},{10,9},{11,1... | collective-permute-start | bytes 2949128 | tf_op jit(solution)/shard_map/ppermute | solution.py:26
  126.2 44.1 %collective-permute-done.4 = f32[6,20,2048]{2,1,0:T(8,128)S(1)} collective-permute-done((f32[6,20,2048]{2,1,0:T(8,128)S(1)}, f32[6,20,2048]{2,1,0:T(8,128)S(1)}, u32[]{:S(2)}, u32[]{:S(2)}) %collective-permute-start.4) | collective-permute-done | bytes 983072 | tf_op jit(solution)/shard_map/ppermute | solution.py:26
  170.5 5.5 %collective-permute-done.5 = f32[6,20,2048]{2,1,0:T(8,128)S(1)} collective-permute-done((f32[6,20,2048]{2,1,0:T(8,128)S(1)}, f32[6,20,2048]{2,1,0:T(8,128)S(1)}, u32[]{:S(2)}, u32[]{:S(2)}) %collective-permute-start.5) | collective-permute-done | bytes 983072 | tf_op jit(solution)/shard_map/ppermute | solution.py:26
  176.4 1.4 copy.32
  177.8 1.9 collective-permute-start.6
  179.7 1.3 copy.34
  181.1 13.9 %collective-permute-start.7 = (f32[16,6,2048]{2,0,1:T(8,128)}, f32[16,6,2048]{2,0,1:T(8,128)}, u32[]{:S(2)}, u32[]{:S(2)}) collective-permute-start(f32[16,6,2048]{2,0,1:T(8,128)} %copy.34), channel_id=1, source_target_pairs={{0,496},{16,0},{32,16},{48,32},{64,48},{80,64},{96,80},{112,96},{1... | collective-permute-start | bytes 2359304 | tf_op jit(solution)/shard_map/ppermute | solution.py:31
  195.0 2.1 copy.28
  197.1 2.1 reshape.211
  199.2 1.2 copy.29
  200.4 2.1 reshape.212
  202.6 1.1 slice.169
  203.6 2.8 %slice_add_fusion.3 = f32[16,6,2048]{2,1,0:T(8,128)} fusion(f32[16,20,2048]{2,1,0:T(8,128)S(1)} %fusion.39, f32[16,6,2048]{2,0,1:T(8,128)} %collective-permute-done.6), kind=kLoop, calls=%fused_computation.53 | loop fusion | flops 196608 | bytes 2359296 | tf_op jit(solution)/shard_map/add | solution.py:129
  206.4 5.4 %scatter-add.16 = f32[16,8,2048]{2,1,0:T(8,128)} dynamic-update-slice(f32[16,8,2048]{2,1,0:T(8,128)} %slice.169, f32[16,6,2048]{2,1,0:T(8,128)} %slice_add_fusion.3, s32[]{:T(128)} %constant.146.clone.1, s32[]{:T(128)} %constant.146.clone.1, s32[]{:T(128)} %constant.146.clone.1) | dynamic-update-slice | bytes 1572868 | tf_op jit(solution)/shard_map/scatter-add | solution.py:129
  211.9 2.1 slice_add_fusion.2
  214.0 1.1 scatter-add.19
  (68 shorter events, 15.2 us)
Async XLA Ops:
  2.7 18.3 %collective-permute-start = (bf16[16,6,2048]{2,1,0:T(8,128)(2,1)S(1)}, bf16[16,6,2048]{2,1,0:T(8,128)(2,1)S(1)}, u32[]{:S(2)}, u32[]{:S(2)}) collective-permute-start(bf16[16,6,2048]{2,1,0:T(8,128)(2,1)S(1)} %get-tuple-element.223), channel_id=1, source_target_pairs={{0,16},{16,32},{32,48},{48,64},{64,80},{80,96},{96,112},{112,128},... | collective-permute-start | bytes 1179656 | tf_op jit(solution)/shard_map/ppermute | solution.py:17
  4.7 18.1 %collective-permute-start.1 = (bf16[16,6,2048]{2,1,0:T(8,128)(2,1)S(1)}, bf16[16,6,2048]{2,1,0:T(8,128)(2,1)S(1)}, u32[]{:S(2)}, u32[]{:S(2)}) collective-permute-start(bf16[16,6,2048]{2,1,0:T(8,128)(2,1)S(1)} %get-tuple-element.224), channel_id=1, source_target_pairs={{16,0},{32,16},{48,32},{64,48},{80,64},{96,80},{112,96},{128,112},... | collective-permute-start | bytes 1179656 | tf_op jit(solution)/shard_map/ppermute | solution.py:18
  16.1 15.5 %copy-start.1 = (bf16[16,8,1024]{2,1,0:T(8,128)(2,1)S(1)}, bf16[16,8,1024]{2,1,0:T(8,128)(2,1)}, u32[]{:S(2)}) copy-start(bf16[16,8,1024]{2,1,0:T(8,128)(2,1)} %param.14) | copy-start | bytes 786436
  24.2 8.2 %copy-start.2 = (bf16[16,8,1024]{2,1,0:T(8,128)(2,1)S(1)}, bf16[16,8,1024]{2,1,0:T(8,128)(2,1)}, u32[]{:S(2)}) copy-start(bf16[16,8,1024]{2,1,0:T(8,128)(2,1)} %param.17) | copy-start | bytes 786436
  24.2 26.6 %collective-permute-start.2 = (bf16[6,20,2048]{2,1,0:T(8,128)(2,1)}, bf16[6,20,2048]{2,1,0:T(8,128)(2,1)S(1)}, u32[]{:S(2)}, u32[]{:S(2)}) collective-permute-start(bf16[6,20,2048]{2,1,0:T(8,128)(2,1)} %get-tuple-element.219), channel_id=1, source_target_pairs={{0,1},{1,2},{2,3},{3,4},{4,5},{5,6},{6,7},{7,8},{8,9},{9,10},{10,1... | collective-permute-start | bytes 1474568 | tf_op jit(solution)/shard_map/ppermute | solution.py:17
  29.1 29.3 %collective-permute-start.3 = (bf16[6,20,2048]{2,1,0:T(8,128)(2,1)}, bf16[6,20,2048]{2,1,0:T(8,128)(2,1)}, u32[]{:S(2)}, u32[]{:S(2)}) collective-permute-start(bf16[6,20,2048]{2,1,0:T(8,128)(2,1)} %get-tuple-element.220), channel_id=1, source_target_pairs={{1,0},{2,1},{3,2},{4,3},{5,4},{6,5},{7,6},{8,7},{9,8},{10,9},{11,1... | collective-permute-start | bytes 1474568 | tf_op jit(solution)/shard_map/ppermute | solution.py:18
  120.0 50.4 %collective-permute-start.4 = (f32[6,20,2048]{2,1,0:T(8,128)S(1)}, f32[6,20,2048]{2,1,0:T(8,128)S(1)}, u32[]{:S(2)}, u32[]{:S(2)}) collective-permute-start(f32[6,20,2048]{2,1,0:T(8,128)S(1)} %get-tuple-element.214), channel_id=1, source_target_pairs={{0,1},{1,2},{2,3},{3,4},{4,5},{5,6},{6,7},{7,8},{8,9},{9,10},{10,1... | collective-permute-start | bytes 2949128 | tf_op jit(solution)/shard_map/ppermute | solution.py:26
  121.9 54.0 %collective-permute-start.5 = (f32[6,20,2048]{2,1,0:T(8,128)S(1)}, f32[6,20,2048]{2,1,0:T(8,128)S(1)}, u32[]{:S(2)}, u32[]{:S(2)}) collective-permute-start(f32[6,20,2048]{2,1,0:T(8,128)S(1)} %get-tuple-element.213), channel_id=1, source_target_pairs={{1,0},{2,1},{3,2},{4,3},{5,4},{6,5},{7,6},{8,7},{9,8},{10,9},{11,1... | collective-permute-start | bytes 2949128 | tf_op jit(solution)/shard_map/ppermute | solution.py:26
  177.8 25.8 %collective-permute-start.6 = (f32[16,6,2048]{2,0,1:T(8,128)}, f32[16,6,2048]{2,0,1:T(8,128)}, u32[]{:S(2)}, u32[]{:S(2)}) collective-permute-start(f32[16,6,2048]{2,0,1:T(8,128)} %copy.32), channel_id=1, source_target_pairs={{0,16},{16,32},{32,48},{48,64},{64,80},{80,96},{96,112},{112,128},... | collective-permute-start | bytes 2359304 | tf_op jit(solution)/shard_map/ppermute | solution.py:31
  181.1 30.8 %collective-permute-start.7 = (f32[16,6,2048]{2,0,1:T(8,128)}, f32[16,6,2048]{2,0,1:T(8,128)}, u32[]{:S(2)}, u32[]{:S(2)}) collective-permute-start(f32[16,6,2048]{2,0,1:T(8,128)} %copy.34), channel_id=1, source_target_pairs={{0,496},{16,0},{32,16},{48,32},{64,48},{80,64},{96,80},{112,96},{1... | collective-permute-start | bytes 2359304 | tf_op jit(solution)/shard_map/ppermute | solution.py:31
  211.9 2.1 copy-start
where the time goes:
time: 217 us; the launch traced here: 216 us
  waiting for transfers between devices  81.4 us (38%)
  local copies, waits for them, and re-layouts  62.3 us (29%)
  starting transfers between devices  41.9 us (19%)
  matrix products  17.9 us (8%)
  other arithmetic  11.4 us (5%)
    ppermute x2, waiting for transfers between devices, passed_along(): return lax.ppermute(block, axis, route)  49.6 us
    ppermute x2, waiting for transfers between devices, extended_2(): before = lax.ppermute(last, axis, up)  22.4 us
    ppermute x2, starting transfers between devices, from_behind(): lax.ppermute(value, axis, [(i, (i + by) % peers) for i in range(peers)])  15.8 us
    reshape x4, local copies, waits for them, and re-layouts, from_groups(): return field.transpose(1, 0, 2, 3).reshape(rows_out, cols_out, -1)  15.1 us
    transpose x4, local copies, waits for them, and re-layouts, from_groups(): return field.transpose(1, 0, 2, 3).reshape(rows_out, cols_out, -1)  13.5 us
    ppermute x2, starting transfers between devices, extended_2(): after = lax.ppermute(leading, axis, down)  13.3 us
    unnamed x12, local copies, waits for them, and re-layouts  10.1 us
    ppermute x2, waiting for transfers between devices, extended_2(): after = lax.ppermute(leading, axis, down)  9.39 us
  transfers between devices with their start and end apart: 8, of which 6 were waited for; matrix products, arithmetic and copies ran while one was open for 10% of the time, Pallas kernels for 0%

commit v1 on v0

v1 whole, which is shorter than its diff:
```python
import functools

import jax
import jax.numpy as jnp
from jax import lax
from jax.experimental import pallas as pl
from jax.experimental.pallas import tpu as pltpu
from jax.sharding import PartitionSpec as P

RADIUS = 6
HEAD = 64
ROWS = 16
COLS = 8
OWN = ROWS * COLS
NN, SS, WW, EE, WC, EC, EXT = 128, 176, 224, 320, 416, 496, 576
LOG2E = 1.4426950408889634
NEG = -1e30
F32, BF16, I32 = jnp.float32, jnp.bfloat16, jnp.int32
MESH = pl.DeviceIdType.MESH
NEIGHBOURS = [(a, b) for a in (-1, 0, 1) for b in (-1, 0, 1) if (a, b) != (0, 0)]


def iota(shape, dim):
    return lax.broadcasted_iota(I32, shape, dim)


def div6(x):
    return (x * 171) >> 10


def ext_coords(e):
    j = e - WW
    r6 = div6(jnp.maximum(j, 0))
    row = r6
    col = j - 6 * r6 - 6
    j = e - EE
    r6 = div6(jnp.maximum(j, 0))
    row = jnp.where(e >= EE, r6, row)
    col = jnp.where(e >= EE, j - 6 * r6 + COLS, col)
    row = jnp.where(e < WW, ROWS + ((e - SS) >> 3), row)
    row = jnp.where(e < SS, ((e - NN) >> 3) - RADIUS, row)
    row = jnp.where(e < NN, e >> 3, row)
    col = jnp.where(e < WW, e & 7, col)
    j = jnp.where(e >= EC, e - EC, e - WC)
    low = j >= 40
    j = jnp.maximum(jnp.where(low, j - 40, j), 0)
    r6 = div6(j)
    ok = (e < WC) | (j < 36)
    row = jnp.where(e >= WC, jnp.where(low, ROWS + r6, r6 - RADIUS), row)
    col = jnp.where(e >= WC, j - 6 * r6 + jnp.where(e >= EC, COLS, -RADIUS), col)
    return row, col, ok


def pack_matrix(first_col):
    i = iota((96, OWN), 0)
    r = div6(i)
    src = r * 8 + (i - 6 * r) + first_col
    return jnp.where(iota((96, OWN), 1) == src, 1.0, 0.0).astype(BF16)


def corner_matrix(first_col):
    i = iota((80, 96), 0)
    low = i >= 40
    j = jnp.where(low, i - 40, i)
    r = div6(j)
    src = r * 8 + (j - 6 * r) + first_col + jnp.where(low, 48, 0)
    src = jnp.where(j < 36, src, -1)
    return jnp.where(iota((80, 96), 1) == src, 1.0, 0.0).astype(BF16)


def dot_t(a, b):
    return lax.dot_general(a, b, (((1,), (1,)), ((), ())), preferred_element_type=F32)


def dot(a, b):
    return jnp.dot(a, b, preferred_element_type=F32)


def kernel(n_lat, n_lon, pairs, q_ref, k_ref, v_ref, c_ref, o_ref, dq_ref, dk_ref, dv_ref,
           ext, snd_side, snd_corner, bias1, bias2, perm, stat_acc, stat_own, stat_in, stat_ext,
           send_sem, recv_sem, stat_send, stat_recv):
    lat, lon = lax.axis_index("lat"), lax.axis_index("lon")
    heads = 2 * pairs
    total_rows = n_lat * ROWS
    first = lat * ROWS
    scale = HEAD ** -0.5

    def device(a, b):
        return {"lat": lax.rem(lat + a + n_lat, n_lat), "lon": lax.rem(lon + b + n_lon, n_lon)}

    barrier = pltpu.get_barrier_semaphore()
    for a, b in NEIGHBOURS:
        pl.semaphore_signal(barrier, inc=1, device_id=device(a, b), device_id_type=MESH)

    def remote(src, dst, sem, to):
        return pltpu.make_async_remote_copy(
            src_ref=src, dst_ref=dst, send_sem=send_sem.at[sem], recv_sem=recv_sem.at[sem],
            device_id=to, device_id_type=MESH)

    def strips(s):
        at = pl.ds(2 * s, 2)
        return [
            remote(ext.at[at, :, pl.ds(0, 48)], ext.at[at, :, pl.ds(SS, 48)], 6 * s, device(-1, 0)),
            remote(ext.at[at, :, pl.ds(80, 48)], ext.at[at, :, pl.ds(NN, 48)], 6 * s + 1, device(1, 0)),
        ]

    def sides(s):
        at = pl.ds(2 * s, 2)
        return [
            remote(snd_side.at[0, at], ext.at[at, :, pl.ds(WW, 96)], 6 * s + 2, device(0, 1)),
            remote(snd_side.at[1, at], ext.at[at, :, pl.ds(EE, 96)], 6 * s + 3, device(0, -1)),
        ]

    def corners(s):
        at = pl.ds(2 * s, 2)
        return [
            remote(snd_corner.at[0, at], ext.at[at, :, pl.ds(WC, 80)], 6 * s + 4, device(0, 1)),
            remote(snd_corner.at[1, at], ext.at[at, :, pl.ds(EC, 80)], 6 * s + 5, device(0, -1)),
        ]

    def start(copies):
        for copy in copies:
            copy.start()

    def pack(s):
        east, west = pack_matrix(2), pack_matrix(0)
        for a, ref in ((2 * s, (k_ref, q_ref)[s]), (2 * s + 1, (v_ref, c_ref)[s])):
            for p in range(pairs):
                block = ref[:, 128 * p:128 * (p + 1)]
                ext[a, p, 0:OWN, :] = block
                snd_side[0, a, p] = dot(east, block).astype(BF16)
                snd_side[1, a, p] = dot(west, block).astype(BF16)

    def pack_corners(s):
        east, west = corner_matrix(2), corner_matrix(0)
        for a in (2 * s, 2 * s + 1):
            for p in range(pairs):
                block = ext[a, p, NN:WW, :]
                snd_corner[0, a, p] = dot(east, block).astype(BF16)
                snd_corner[1, a, p] = dot(west, block).astype(BF16)

    pack(0)
    pl.semaphore_wait(barrier, len(NEIGHBOURS))
    start(strips(0))
    start(sides(0))
    pack(1)
    start(strips(1))
    start(sides(1))

    row, col, ok = ext_coords(iota((OWN, EXT), 1))
    own = iota((OWN, EXT), 0)
    near = (jnp.abs(col - (own & 7)) <= RADIUS) & ok
    own_row = first + (own >> 3)
    ext_row = first + row
    begin = jnp.clip(own_row - RADIUS, 0, total_rows - 2 * RADIUS - 1)
    inside = near & (ext_row >= begin) & (ext_row <= begin + 2 * RADIUS)
    bias1[...] = jnp.where(inside, 0.0, NEG)
    begin = jnp.clip(ext_row - RADIUS, 0, total_rows - 2 * RADIUS - 1)
    inside = near & (own_row >= begin) & (own_row <= begin + 2 * RADIUS)
    inside = inside & (ext_row >= 0) & (ext_row < total_rows)
    bias2[...] = jnp.where(inside, 0.0, NEG)

    row, col, ok = ext_coords(iota((8, EXT), 1))
    above, below = row < 0, row >= ROWS
    left, right = col < 0, col >= COLS
    part = 4 + jnp.where(above, -3, 0) + jnp.where(below, 3, 0) + jnp.where(left, -1, 0) + jnp.where(right, 1, 0)
    src = part * OWN + (row & (ROWS - 1)) * 8 + (col & (COLS - 1))
    src = jnp.where(ok, src, -1)[0:1]
    for b in range(9):
        at = iota((OWN, EXT), 0) + b * OWN
        perm[b * OWN:(b + 1) * OWN, :] = jnp.where(at == src, 1.0, 0.0).astype(BF16)

    for copy in strips(0):
        copy.wait_recv()
    pack_corners(0)
    start(corners(0))
    for copy in strips(1):
        copy.wait_recv()
    pack_corners(1)
    start(corners(1))

    lane = iota((1, 128), 1)
    lo = jnp.where(lane < HEAD, 1.0, 0.0).astype(BF16)
    hi = jnp.where(lane < HEAD, 0.0, 1.0).astype(BF16)
    lower = iota((OWN, 128), 1) < HEAD

    def by_head(x):
        return jnp.concatenate([x * lo, x * hi], axis=0)

    def merged(x):
        return jnp.where(lower, x[:OWN], x[OWN:])

    def lanes(p):
        return pl.ds(pl.multiple_of(p * 128, 128), 128)

    for copy in sides(0) + corners(0):
        copy.wait_recv()

    stat_acc[...] = jnp.zeros_like(stat_acc)

    def forward(p, carry):
        kx, vx = ext[0, p], ext[1, p]
        qs = by_head(ext[2, p, 0:OWN, :])
        cs = by_head(ext[3, p, 0:OWN, :])
        s = dot_t(qs, kx)
        dw = dot_t(cs, vx)
        rounded, grads = [], []
        lane_at = iota((OWN, 128), 1)
        acc = stat_acc[...]
        for h in range(2):
            part = slice(h * OWN, (h + 1) * OWN)
            t = s[part] * (scale * LOG2E) + bias1[...]
            m = jnp.max(t, axis=1, keepdims=True)
            e = jnp.exp2(t - m)
            total = jnp.sum(e, axis=1, keepdims=True)
            w = e * (1.0 / total)
            rounded.append(w.astype(BF16))
            g = dw[part]
            delta = jnp.sum(w * g, axis=1, keepdims=True)
            grads.append((w * (g - delta)).astype(BF16))
            acc = jnp.where(lane_at == 2 * p + h, m + jnp.log2(total), acc)
            acc = jnp.where(lane_at == heads + 2 * p + h, delta, acc)
        stat_acc[...] = acc
        o = dot(jnp.concatenate(rounded, axis=0), vx)
        dq = dot(jnp.concatenate(grads, axis=0), kx)
        o_ref[:, lanes(p)] = merged(o).astype(BF16)
        dq_ref[:, lanes(p)] = (merged(dq) * scale).astype(BF16)
        return carry

    lax.fori_loop(0, pairs, forward, 0)

    stat_own[...] = stat_acc[...].T[0:2 * heads]

    def stat_copy(i, to):
        return pltpu.make_async_remote_copy(
            src_ref=stat_own, dst_ref=stat_in.at[i], send_sem=stat_send.at[i], recv_sem=stat_recv.at[i],
            device_id=to, device_id_type=MESH)

    stats = [stat_copy(i, device(-a, -b)) for i, (a, b) in enumerate(NEIGHBOURS)]
    start(stats)

    for copy in sides(1) + corners(1):
        copy.wait_recv()
    for copy in stats:
        copy.wait_recv()

    blocks = [stat_in[i] for i in range(8)]
    blocks = blocks[:4] + [stat_own[...]] + blocks[4:]
    x = jnp.concatenate(blocks, axis=1)
    x1 = x.astype(BF16)
    rest = x - x1.astype(F32)
    x2 = rest.astype(BF16)
    x3 = (rest - x2.astype(F32)).astype(BF16)
    y = dot(jnp.concatenate([x1, x2, x3], axis=0), perm[...])
    y = (y[0:2 * heads] + y[2 * heads:4 * heads]) + y[4 * heads:6 * heads]
    for i in range(2 * heads):
        stat_ext[i] = y[i:i + 1]

    def backward(p, carry):
        qx, cx = ext[2, p], ext[3, p]
        ks = by_head(ext[0, p, 0:OWN, :])
        vs = by_head(ext[1, p, 0:OWN, :])
        s = dot_t(ks, qx)
        dw = dot_t(vs, cx)
        rounded, grads = [], []
        for h in range(2):
            part = slice(h * OWN, (h + 1) * OWN)
            norm = stat_ext[2 * p + h]
            delta = stat_ext[heads + 2 * p + h]
            w = jnp.exp2(s[part] * (scale * LOG2E) + bias2[...] - norm)
            rounded.append(w.astype(BF16))
            grads.append((w * (dw[part] - delta)).astype(BF16))
        dv = dot(jnp.concatenate(rounded, axis=0), cx)
        dk = dot(jnp.concatenate(grads, axis=0), qx)
        dv_ref[:, lanes(p)] = merged(dv).astype(BF16)
        dk_ref[:, lanes(p)] = (merged(dk) * scale).astype(BF16)
        return carry

    lax.fori_loop(0, pairs, backward, 0)

    for s in range(2):
        for copy in strips(s) + sides(s) + corners(s):
            copy.wait_send()
    for copy in stats:
        copy.wait_send()


def solution(mesh):
    n_lat, n_lon = mesh.shape["lat"], mesh.shape["lon"]

    def shards(queries, keys, values, cotangent):
        width = queries.shape[2]
        pairs = width // 128
        heads = 2 * pairs
        flat = [x.reshape(OWN, width) for x in (queries, keys, values, cotangent)]
        outs = pl.pallas_call(
            functools.partial(kernel, n_lat, n_lon, pairs),
            out_shape=[jax.ShapeDtypeStruct((OWN, width), BF16)] * 4,
            in_specs=[pl.BlockSpec(memory_space=pltpu.VMEM)] * 4,
            out_specs=[pl.BlockSpec(memory_space=pltpu.VMEM)] * 4,
            scratch_shapes=[
                pltpu.VMEM((4, pairs, EXT, 128), BF16),
                pltpu.VMEM((2, 4, pairs, 96, 128), BF16),
                pltpu.VMEM((2, 4, pairs, 80, 128), BF16),
                pltpu.VMEM((OWN, EXT), F32),
                pltpu.VMEM((OWN, EXT), F32),
                pltpu.VMEM((9 * OWN, EXT), BF16),
                pltpu.VMEM((OWN, 128), F32),
                pltpu.VMEM((2 * heads, OWN), F32),
                pltpu.VMEM((8, 2 * heads, OWN), F32),
                pltpu.VMEM((2 * heads, 1, EXT), F32),
                pltpu.SemaphoreType.DMA((12,)),
                pltpu.SemaphoreType.DMA((12,)),
                pltpu.SemaphoreType.DMA((8,)),
                pltpu.SemaphoreType.DMA((8,)),
            ],
            compiler_params=pltpu.CompilerParams(
                collective_id=0, has_side_effects=True, vmem_limit_bytes=48 * 1024 * 1024),
        )(*flat)
        return tuple(x.reshape(ROWS, COLS, width) for x in outs)

    spec = P("lat", "lon", None)
    return jax.shard_map(shards, mesh=mesh, in_specs=(spec,) * 4, out_specs=(spec,) * 4, check_vma=False)
```

time: 217 us -> 69 us (0.32)
  waiting for transfers between devices: 81.4 us -> 0 us
  Pallas kernels: 0 us -> 61.5 us
  local copies, waits for them, and re-layouts: 62.3 us -> 6.6 us
  starting transfers between devices: 41.9 us -> 0 us
  matrix products: 17.9 us -> 0 us
  other arithmetic: 11.4 us -> 0 us
    ppermute x8 -> x0, waiting for transfers between devices: 81.4 us -> none  [the longest x2 49.6 us: passed_along(): return lax.ppermute(block, axis, route)]
    pallas_call x0 -> x1, Pallas kernels: none -> 61.5 us  [shards(): pl.pallas_call(functools.partial(kernel, n_lat, n_lon, pairs), out_shape=...]
    ppermute x8 -> x0, starting transfers between devices: 41.9 us -> none  [the longest x2 15.8 us: from_behind(): lax.ppermute(value, axis, [(i, (i + by) % peers) for i in range(peers)])]
    reshape x8 -> x0, local copies, waits for them, and re-layouts: 23.7 us -> none  [the longest x4 15.1 us: from_groups(): return field.transpose(1, 0, 2, 3).reshape(rows_out, cols_out, -1)]
    dot_general x24 -> x0, matrix products: 17.9 us -> none  [the longest x4 4.9 us: with_partials(): jnp.einsum('hne,nhd->ehd', rounded, items[3], preferred_element_type=jnp....]
    transpose x4 -> x0, local copies, waits for them, and re-layouts: 13.5 us -> none  [from_groups(): return field.transpose(1, 0, 2, 3).reshape(rows_out, cols_out, -1)]
    slice x9 -> x0, local copies, waits for them, and re-layouts: 6.81 us -> none  [the longest x2 1.54 us: shards(): west_rim = middle[:, :RADIUS]]
    scatter-add x2 -> x0, local copies, waits for them, and re-layouts: 6.51 us -> none  [the longest x1 5.42 us: shards(): folded = folded.at[:, :RADIUS].add(from_west)]
  transfers between devices with their start and end apart: 8 -> 0, of which waited for: 6 -> 0; matrix products, arithmetic and copies ran while one was open for 10% -> 0% of each run, Pallas kernels for 0% -> 0%
where the time goes in v1:
time: 69 us; the launch traced here: 68.7 us
  Pallas kernels  61.5 us (89%)
  local copies, waits for them, and re-layouts  6.6 us (10%)
    pallas_call x1, Pallas kernels, shards(): pl.pallas_call(functools.partial(kernel, n_lat, n_lon, pairs), out_shape=...  61.5 us
    unnamed x12, local copies, waits for them, and re-layouts  6.6 us

profile of v1, /device:TPU:22, one launch (start us, length us, event | category | flops | bytes accessed | tf_op | source)
XLA Modules:
  0.0 68.7 jit_solution(4316132768392844377)
XLA Ops:
  0.6 0.0 copy-start
  0.6 0.9 %copy-done = bf16[16,8,1024]{2,1,0:T(8,128)(2,1)S(1)} copy-done((bf16[16,8,1024]{2,1,0:T(8,128)(2,1)S(1)}, bf16[16,8,1024]{2,1,0:T(8,128)(2,1)}, u32[]{:S(2)}) %copy-start) | copy-done | bytes 262168
  1.6 0.0 copy-start.1
  1.6 0.9 %copy-done.1 = bf16[16,8,1024]{2,1,0:T(8,128)(2,1)S(1)} copy-done((bf16[16,8,1024]{2,1,0:T(8,128)(2,1)S(1)}, bf16[16,8,1024]{2,1,0:T(8,128)(2,1)}, u32[]{:S(2)}) %copy-start.1) | copy-done | bytes 262168
  2.5 0.0 copy-start.2
  2.5 0.9 %copy-done.2 = bf16[16,8,1024]{2,1,0:T(8,128)(2,1)S(1)} copy-done((bf16[16,8,1024]{2,1,0:T(8,128)(2,1)S(1)}, bf16[16,8,1024]{2,1,0:T(8,128)(2,1)}, u32[]{:S(2)}) %copy-start.2) | copy-done | bytes 262168
  3.5 0.0 copy-start.3
  3.5 0.9 %copy-done.3 = bf16[16,8,1024]{2,1,0:T(8,128)(2,1)S(1)} copy-done((bf16[16,8,1024]{2,1,0:T(8,128)(2,1)S(1)}, bf16[16,8,1024]{2,1,0:T(8,128)(2,1)}, u32[]{:S(2)}) %copy-start.3) | copy-done | bytes 262168
  4.4 61.5 %shard_map.75 = (bf16[128,1024]{1,0:T(8,128)(2,1)S(1)}, bf16[128,1024]{1,0:T(8,128)(2,1)S(1)}, bf16[128,1024]{1,0:T(8,128)(2,1)S(1)}, bf16[128,1024]{1,0:T(8,128)(2,1)S(1)}) custom-call(bf16[128,1024]{1,0:T(8,128)(2,1)S(1)} %bitcast.12, bf16[128,1024]{1,0:T(8,128)(2,1)S(1)} %bitcast.13, bf16[128,1024]{1,0:T(8,128)(2,1)S(1)} %bitcast.14, ...), custom_call_target="tpu_custom_call" | custom-call | tf_op jit(solution)/shard_map/pallas_call | solution.py:296
  65.9 0.7 %copy.12 = bf16[16,8,1024]{2,1,0:T(8,128)(2,1)} copy(bf16[16,8,1024]{2,1,0:T(8,128)(2,1)S(1)} %bitcast.11) | data formatting | bytes 524288
  66.6 0.7 %copy.13 = bf16[16,8,1024]{2,1,0:T(8,128)(2,1)} copy(bf16[16,8,1024]{2,1,0:T(8,128)(2,1)S(1)} %bitcast.10) | data formatting | bytes 524288
  67.3 0.7 %copy.14 = bf16[16,8,1024]{2,1,0:T(8,128)(2,1)} copy(bf16[16,8,1024]{2,1,0:T(8,128)(2,1)S(1)} %bitcast.9) | data formatting | bytes 524288
  68.0 0.7 %copy.15 = bf16[16,8,1024]{2,1,0:T(8,128)(2,1)} copy(bf16[16,8,1024]{2,1,0:T(8,128)(2,1)S(1)} %bitcast.8) | data formatting | bytes 524288
Async XLA Ops:
  0.6 1.0 %copy-start = (bf16[16,8,1024]{2,1,0:T(8,128)(2,1)S(1)}, bf16[16,8,1024]{2,1,0:T(8,128)(2,1)}, u32[]{:S(2)}) copy-start(bf16[16,8,1024]{2,1,0:T(8,128)(2,1)} %param.4) | copy-start | bytes 786436
  1.6 0.9 %copy-start.1 = (bf16[16,8,1024]{2,1,0:T(8,128)(2,1)S(1)}, bf16[16,8,1024]{2,1,0:T(8,128)(2,1)}, u32[]{:S(2)}) copy-start(bf16[16,8,1024]{2,1,0:T(8,128)(2,1)} %param.5) | copy-start | bytes 786436
  2.5 0.9 %copy-start.2 = (bf16[16,8,1024]{2,1,0:T(8,128)(2,1)S(1)}, bf16[16,8,1024]{2,1,0:T(8,128)(2,1)}, u32[]{:S(2)}) copy-start(bf16[16,8,1024]{2,1,0:T(8,128)(2,1)} %param.6) | copy-start | bytes 786436
  3.5 0.9 %copy-start.3 = (bf16[16,8,1024]{2,1,0:T(8,128)(2,1)S(1)}, bf16[16,8,1024]{2,1,0:T(8,128)(2,1)}, u32[]{:S(2)}) copy-start(bf16[16,8,1024]{2,1,0:T(8,128)(2,1)} %param.7) | copy-start | bytes 786436

commit v2 on v1

v2 whole, which is shorter than its diff:
```python
import functools

import jax
import jax.numpy as jnp
from jax import lax
from jax.experimental import pallas as pl
from jax.experimental.pallas import tpu as pltpu
from jax.sharding import PartitionSpec as P

RADIUS = 6
HEAD = 64
ROWS = 16
COLS = 8
OWN = ROWS * COLS
HALF = OWN // 2
NN, CN, MID, WW, EE, SS, CS, EXT = 0, 48, 128, 256, 352, 448, 496, 576
SPAN = 448
SEGMENTS = [
    (0, 8, -6, 0, 48), (48, 6, -6, -6, 36), (88, 6, -6, 8, 36), (128, 8, 0, 0, 128), (256, 6, 0, -6, 96),
    (352, 6, 0, 8, 96), (448, 8, 16, 0, 48), (496, 6, 16, 8, 36), (536, 6, 16, -6, 36),
]
XS = 4
LOG2E = 1.4426950408889634
NEG = -1e30
F32, BF16, I32 = jnp.float32, jnp.bfloat16, jnp.int32
MESH = pl.DeviceIdType.MESH
NEIGHBOURS = [(a, b) for a in (-1, 0, 1) for b in (-1, 0, 1) if (a, b) != (0, 0)]
GREETED = NEIGHBOURS + [(a, 0) for a in (-4, -3, -2, 2, 3, 4)]


def iota(shape, dim):
    return lax.broadcasted_iota(I32, shape, dim)


def div6(x):
    return (x * 171) >> 10


def ext_coords(e):
    row = col = ok = None
    for first, wide, row0, col0, count in SEGMENTS:
        j = jnp.maximum(e - first, 0)
        r = (j >> 3) if wide == 8 else div6(j)
        c = j - wide * r + col0
        r = r + row0
        good = jnp.where(j < count, 1, 0)
        if row is None:
            row, col, ok = r, c, good
        else:
            row = jnp.where(e >= first, r, row)
            col = jnp.where(e >= first, c, col)
            ok = jnp.where(e >= first, good, ok)
    return row, col, ok > 0


def pack_matrix(first_col):
    i = iota((96, OWN), 0)
    r = div6(i)
    src = r * 8 + (i - 6 * r) + first_col
    return jnp.where(iota((96, OWN), 1) == src, 1.0, 0.0).astype(BF16)


def corner_matrix(first_col, swapped):
    i = iota((80, 96), 0)
    second = i >= 40
    j = jnp.where(second, i - 40, i)
    r = div6(j)
    from_below = jnp.where(second, 0, 48) if swapped else jnp.where(second, 48, 0)
    src = r * 8 + (j - 6 * r) + first_col + from_below
    src = jnp.where(j < 36, src, -1)
    return jnp.where(iota((80, 96), 1) == src, 1.0, 0.0).astype(BF16)


def dot_t(a, b):
    return lax.dot_general(a, b, (((1,), (1,)), ((), ())), preferred_element_type=F32)


def dot(a, b):
    return jnp.dot(a, b, preferred_element_type=F32)


def kernel(n_lat, n_lon, pairs, q_hbm, k_hbm, v_hbm, c_hbm, o_ref, dq_ref, dk_ref, dv_ref,
           inputs, ext, snd_side, snd_corner, rcv_corner, relay, bias1, bias2, perm, stat_acc, stat_own, stat_in,
           stat_ext, in_sem, side_s, side_r, corner_s, corner_r, strip_s, strip_r, relay_r, pass_s,
           stat_s, stat_r):
    lat, lon = lax.axis_index("lat"), lax.axis_index("lon")
    x = lax.rem(lat, XS)
    heads = 2 * pairs
    half = pairs // 2
    total_rows = n_lat * ROWS
    first = lat * ROWS
    scale = HEAD ** -0.5

    def device(a, b):
        return {"lat": lax.rem(lat + a + n_lat, n_lat), "lon": lax.rem(lon + b + n_lon, n_lon)}

    barrier = pltpu.get_barrier_semaphore()
    for a, b in GREETED:
        pl.semaphore_signal(barrier, inc=1, device_id=device(a, b), device_id_type=MESH)

    loads = [pltpu.make_async_copy(ref, inputs.at[i], in_sem.at[i])
             for i, ref in enumerate((k_hbm, v_hbm, q_hbm, c_hbm))]
    for load in loads:
        load.start()

    def remote(src, dst, send, recv, to):
        return pltpu.make_async_remote_copy(
            src_ref=src, dst_ref=dst, send_sem=send, recv_sem=recv, device_id=to, device_id_type=MESH)

    def arrays(c):
        return pl.ds(2 * (c // 2), 2)

    def heads_of(c):
        return pl.ds(half * (c % 2), half)

    def strip(c, d):
        src = ext.at[arrays(c), heads_of(c), pl.ds(MID + 80 if d == 0 else MID, 48)]
        dst = ext.at[arrays(c), heads_of(c), pl.ds(NN if d == 0 else SS, 48)]
        return remote(src, dst, strip_s.at[c, d, 0], strip_r.at[c, d, 0], device(1 if d == 0 else -1, 0))

    def part(c, d, j):
        at = (arrays(c), half * (c % 2) + j)
        src = ext.at[*at, pl.ds(MID + 80 if d == 0 else MID, 48)]
        to = device(1 + j, 0) if d == 0 else device(-4 + j, 0)
        if j == (0 if d == 0 else XS - 1):
            dst = ext.at[*at, pl.ds(NN if d == 0 else SS, 48)]
            return remote(src, dst, strip_s.at[c, d, j], strip_r.at[c, d, j], to)
        return remote(src, relay.at[c, d], strip_s.at[c, d, j], relay_r.at[c, d], to)

    def passed(c, d):
        dst = ext.at[arrays(c), half * (c % 2) + x, pl.ds(NN if d == 0 else SS, 48)]
        return remote(relay.at[c, d], dst, pass_s.at[c, d], strip_r.at[c, d, x],
                      device(-x, 0) if d == 0 else device(XS - 1 - x, 0))

    def landed(c, d, j):
        dst = ext.at[arrays(c), half * (c % 2) + j, pl.ds(NN if d == 0 else SS, 48)]
        return remote(relay.at[c, d], dst, pass_s.at[c, d], strip_r.at[c, d, j], device(1, 0))

    last = (XS - 1, 0)

    def start_strips(c):
        for d in range(2):
            @pl.when(x != last[d])
            def _():
                strip(c, d).start()

            @pl.when(x == last[d])
            def _():
                for j in range(XS):
                    part(c, d, j).start()

    def pass_on(c):
        for d in range(2):
            @pl.when(x != last[1 - d])
            def _():
                part(c, d, 1).wait_recv()
                passed(c, d).start()

    def wait_strips(c):
        for d in range(2):
            @pl.when(x != last[1 - d])
            def _():
                strip(c, d).wait_recv()

            @pl.when(x == last[1 - d])
            def _():
                for j in range(XS):
                    landed(c, d, j).wait_recv()

    def sent_strips(c):
        for d in range(2):
            @pl.when(x != last[d])
            def _():
                strip(c, d).wait_send()

            @pl.when(x == last[d])
            def _():
                for j in range(XS):
                    part(c, d, j).wait_send()

            @pl.when(x != last[1 - d])
            def _():
                passed(c, d).wait_send()

    def sides(c):
        return [remote(snd_side.at[i, arrays(c), heads_of(c)], ext.at[arrays(c), heads_of(c), pl.ds(to, 96)],
                       side_s.at[c, i], side_r.at[c, i], device(0, b))
                for i, (to, b) in enumerate(((WW, 1), (EE, -1)))]

    def corners(c):
        return [remote(snd_corner.at[i, arrays(c), heads_of(c)], rcv_corner.at[i, arrays(c), heads_of(c)],
                       corner_s.at[c, i], corner_r.at[c, i], device(0, b))
                for i, b in enumerate((1, -1))]

    def start(copies):
        for copy in copies:
            copy.start()

    def pack(s):
        east, west = pack_matrix(2), pack_matrix(0)
        for a in (2 * s, 2 * s + 1):
            for p in range(pairs):
                block = inputs[a, :, 128 * p:128 * (p + 1)]
                ext[a, p, MID:MID + OWN, :] = block
                snd_side[0, a, p] = dot(east, block).astype(BF16)
                snd_side[1, a, p] = dot(west, block).astype(BF16)

    def pack_corners(c):
        east, west = corner_matrix(2, False), corner_matrix(0, True)
        for a in (2 * (c // 2), 2 * (c // 2) + 1):
            for p in range(half * (c % 2), half * (c % 2) + half):
                block = jnp.concatenate([ext[a, p, NN:NN + 48, :], ext[a, p, SS:SS + 48, :]], axis=0)
                snd_corner[0, a, p] = dot(east, block).astype(BF16)
                snd_corner[1, a, p] = dot(west, block).astype(BF16)

    def place_corners(c):
        for copy in corners(c):
            copy.wait_recv()
        early = iota((80, 128), 0) < 40
        one = jnp.where(early, 1.0, 0.0).astype(BF16)
        two = jnp.where(early, 0.0, 1.0).astype(BF16)
        for a in (2 * (c // 2), 2 * (c // 2) + 1):
            for p in range(half * (c % 2), half * (c % 2) + half):
                w, e = rcv_corner[0, a, p], rcv_corner[1, a, p]
                ext[a, p, CN:CN + 80, :] = w * one + e * two
                ext[a, p, CS:CS + 80, :] = e * one + w * two

    loads[0].wait()
    loads[1].wait()
    pack(0)
    pl.semaphore_wait(barrier, len(GREETED))
    start_strips(0)
    start(sides(0))
    start_strips(1)
    start(sides(1))
    loads[2].wait()
    loads[3].wait()
    pack(1)
    start_strips(2)
    start_strips(3)
    pass_on(0)

    row, col, ok = ext_coords(iota((8, EXT), 1))
    row, col, ok = row[0:1], col[0:1], jnp.where(ok, 1, 0)[0:1]
    for i in range(2):
        e = slice(128 * i, 128 * i + SPAN)
        token = iota((HALF, SPAN), 0) + HALF * i
        near = (jnp.abs(col[:, e] - (token & 7)) <= RADIUS) & (ok[:, e] > 0)
        own_row = first + (token >> 3)
        ext_row = first + row[:, e]
        begin = jnp.clip(own_row - RADIUS, 0, total_rows - 2 * RADIUS - 1)
        inside = near & (ext_row >= begin) & (ext_row <= begin + 2 * RADIUS)
        bias1[HALF * i:HALF * (i + 1), :] = jnp.where(inside, 0.0, NEG)
        begin = jnp.clip(ext_row - RADIUS, 0, total_rows - 2 * RADIUS - 1)
        inside = near & (own_row >= begin) & (own_row <= begin + 2 * RADIUS)
        inside = inside & (ext_row >= 0) & (ext_row < total_rows)
        bias2[HALF * i:HALF * (i + 1), :] = jnp.where(inside, 0.0, NEG)

    pass_on(1)
    wait_strips(0)
    pack_corners(0)
    start(corners(0))
    wait_strips(1)
    pack_corners(1)
    start(corners(1))
    start(sides(2))
    start(sides(3))

    up, down = jnp.where(row < 0, -3, 0), jnp.where(row >= ROWS, 3, 0)
    left, right = jnp.where(col < 0, -1, 0), jnp.where(col >= COLS, 1, 0)
    src = (4 + up + down + left + right) * OWN + (row & (ROWS - 1)) * 8 + (col & (COLS - 1))
    src = jnp.where(ok > 0, src, -1)
    for b in range(9):
        at = iota((OWN, EXT), 0) + b * OWN
        perm[b * OWN:(b + 1) * OWN, :] = jnp.where(at == src, 1.0, 0.0).astype(BF16)

    lane = iota((1, 128), 1)
    lo = jnp.where(lane < HEAD, 1.0, 0.0).astype(BF16)
    hi = jnp.where(lane < HEAD, 0.0, 1.0).astype(BF16)
    lower = iota((HALF, 128), 1) < HEAD

    def by_head(v):
        return jnp.concatenate([v * lo, v * hi], axis=0)

    def merged(v):
        return jnp.where(lower, v[:HALF], v[HALF:])

    def lanes(p):
        return pl.ds(pl.multiple_of(p * 128, 128), 128)

    stat_acc[...] = jnp.zeros_like(stat_acc)

    def forward(p, carry):
        for i in range(2):
            mine = slice(MID + HALF * i, MID + HALF * (i + 1))
            rows = slice(HALF * i, HALF * (i + 1))
            span = slice(128 * i, 128 * i + SPAN)
            kx, vx = ext[0, p, span, :], ext[1, p, span, :]
            s = dot_t(by_head(ext[2, p, mine, :]), kx)
            dw = dot_t(by_head(ext[3, p, mine, :]), vx)
            bias = bias1[rows, :]
            acc = stat_acc[rows, :]
            lane_at = iota((HALF, 128), 1)
            rounded, grads = [], []
            for h in range(2):
                of = slice(h * HALF, (h + 1) * HALF)
                t = s[of] * (scale * LOG2E) + bias
                m = jnp.max(t, axis=1, keepdims=True)
                e = jnp.exp2(t - m)
                total = jnp.sum(e, axis=1, keepdims=True)
                w = e * (1.0 / total)
                rounded.append(w.astype(BF16))
                g = dw[of]
                delta = jnp.sum(w * g, axis=1, keepdims=True)
                grads.append((w * (g - delta)).astype(BF16))
                acc = jnp.where(lane_at == 2 * p + h, m + jnp.log2(total), acc)
                acc = jnp.where(lane_at == heads + 2 * p + h, delta, acc)
            stat_acc[rows, :] = acc
            o = dot(jnp.concatenate(rounded, axis=0), vx)
            dq = dot(jnp.concatenate(grads, axis=0), kx)
            o_ref[rows, lanes(p)] = merged(o).astype(BF16)
            dq_ref[rows, lanes(p)] = (merged(dq) * scale).astype(BF16)
        return carry

    def backward(p, carry):
        for i in range(2):
            mine = slice(MID + HALF * i, MID + HALF * (i + 1))
            rows = slice(HALF * i, HALF * (i + 1))
            span = slice(128 * i, 128 * i + SPAN)
            qx, cx = ext[2, p, span, :], ext[3, p, span, :]
            s = dot_t(by_head(ext[0, p, mine, :]), qx)
            dw = dot_t(by_head(ext[1, p, mine, :]), cx)
            bias = bias2[rows, :]
            rounded, grads = [], []
            for h in range(2):
                of = slice(h * HALF, (h + 1) * HALF)
                norm = stat_ext[2 * p + h][:, span]
                delta = stat_ext[heads + 2 * p + h][:, span]
                w = jnp.exp2(s[of] * (scale * LOG2E) + bias - norm)
                rounded.append(w.astype(BF16))
                grads.append((w * (dw[of] - delta)).astype(BF16))
            dv = dot(jnp.concatenate(rounded, axis=0), cx)
            dk = dot(jnp.concatenate(grads, axis=0), qx)
            dv_ref[rows, lanes(p)] = merged(dv).astype(BF16)
            dk_ref[rows, lanes(p)] = (merged(dk) * scale).astype(BF16)
        return carry

    def wait_sides(c):
        for copy in sides(c):
            copy.wait_recv()

    wait_sides(0)
    place_corners(0)
    lax.fori_loop(0, half, forward, 0)
    pass_on(2)
    pass_on(3)
    wait_strips(2)
    pack_corners(2)
    start(corners(2))
    wait_sides(1)
    place_corners(1)
    lax.fori_loop(half, pairs, forward, 0)

    stat_own[...] = stat_acc[...].T[0:2 * heads]
    stats = [remote(stat_own, stat_in.at[i], stat_s.at[i], stat_r.at[i], device(-a, -b))
             for i, (a, b) in enumerate(NEIGHBOURS)]
    start(stats)
    wait_strips(3)
    pack_corners(3)
    start(corners(3))

    for copy in stats:
        copy.wait_recv()
    blocks = [stat_in[i] for i in range(8)]
    blocks = blocks[:4] + [stat_own[...]] + blocks[4:]
    whole = jnp.concatenate(blocks, axis=1)
    x1 = whole.astype(BF16)
    rest = whole - x1.astype(F32)
    x2 = rest.astype(BF16)
    x3 = (rest - x2.astype(F32)).astype(BF16)
    y = dot(jnp.concatenate([x1, x2, x3], axis=0), perm[...])
    y = (y[0:2 * heads] + y[2 * heads:4 * heads]) + y[4 * heads:6 * heads]
    for i in range(2 * heads):
        stat_ext[i] = y[i:i + 1]

    wait_sides(2)
    place_corners(2)
    lax.fori_loop(0, half, backward, 0)
    wait_sides(3)
    place_corners(3)
    lax.fori_loop(half, pairs, backward, 0)

    for c in range(4):
        sent_strips(c)
        for copy in sides(c) + corners(c):
            copy.wait_send()
    for copy in stats:
        copy.wait_send()


def solution(mesh):
    n_lat, n_lon = mesh.shape["lat"], mesh.shape["lon"]

    def shards(queries, keys, values, cotangent):
        width = queries.shape[2]
        pairs = width // 128
        heads = 2 * pairs
        flat = [x.reshape(OWN, width) for x in (queries, keys, values, cotangent)]
        dma = pltpu.SemaphoreType.DMA
        outs = pl.pallas_call(
            functools.partial(kernel, n_lat, n_lon, pairs),
            out_shape=[jax.ShapeDtypeStruct((OWN, width), BF16)] * 4,
            in_specs=[pl.BlockSpec(memory_space=pltpu.HBM)] * 4,
            out_specs=[pl.BlockSpec(memory_space=pltpu.VMEM)] * 4,
            scratch_shapes=[
                pltpu.VMEM((4, OWN, width), BF16),
                pltpu.VMEM((4, pairs, EXT, 128), BF16),
                pltpu.VMEM((2, 4, pairs, 96, 128), BF16),
                pltpu.VMEM((2, 4, pairs, 80, 128), BF16),
                pltpu.VMEM((2, 4, pairs, 80, 128), BF16),
                pltpu.VMEM((4, 2, 2, 48, 128), BF16),
                pltpu.VMEM((OWN, SPAN), F32),
                pltpu.VMEM((OWN, SPAN), F32),
                pltpu.VMEM((9 * OWN, EXT), BF16),
                pltpu.VMEM((OWN, 128), F32),
                pltpu.VMEM((2 * heads, OWN), F32),
                pltpu.VMEM((8, 2 * heads, OWN), F32),
                pltpu.VMEM((2 * heads, 1, EXT), F32),
                dma((4,)), dma((4, 2)), dma((4, 2)), dma((4, 2)), dma((4, 2)),
                dma((4, 2, XS)), dma((4, 2, XS)), dma((4, 2)), dma((4, 2)), dma((8,)), dma((8,)),
            ],
            compiler_params=pltpu.CompilerParams(
                collective_id=0, has_side_effects=True, vmem_limit_bytes=48 * 1024 * 1024),
        )(*flat)
        return tuple(x.reshape(ROWS, COLS, width) for x in outs)

    spec = P("lat", "lon", None)
    return jax.shard_map(shards, mesh=mesh, in_specs=(spec,) * 4, out_specs=(spec,) * 4, check_vma=False)
```

time: 69 us -> 72.5 us (1.051)
  the two profiles are of different devices: /device:TPU:22 before, /device:TPU:1 now
where the time goes in v2:
time: 72.5 us; the launch traced here: 72.3 us
  Pallas kernels  65 us (90%)
  local copies, waits for them, and re-layouts  6.6 us (9%)
    pallas_call x1, Pallas kernels, shards(): pl.pallas_call(functools.partial(kernel, n_lat, n_lon, pairs), out_shape=...  65 us
    unnamed x12, local copies, waits for them, and re-layouts  6.6 us

profile of v2, /device:TPU:1, one launch (start us, length us, event | category | flops | bytes accessed | tf_op | source)
XLA Modules:
  0.0 72.3 jit_solution(16445988972362322515)
XLA Ops:
  0.6 0.0 copy-start
  0.6 0.9 %copy-done = bf16[16,8,1024]{2,1,0:T(8,128)(2,1)S(1)} copy-done((bf16[16,8,1024]{2,1,0:T(8,128)(2,1)S(1)}, bf16[16,8,1024]{2,1,0:T(8,128)(2,1)}, u32[]{:S(2)}) %copy-start) | copy-done | bytes 262168
  1.6 0.0 copy-start.1
  1.6 0.9 %copy-done.1 = bf16[16,8,1024]{2,1,0:T(8,128)(2,1)S(1)} copy-done((bf16[16,8,1024]{2,1,0:T(8,128)(2,1)S(1)}, bf16[16,8,1024]{2,1,0:T(8,128)(2,1)}, u32[]{:S(2)}) %copy-start.1) | copy-done | bytes 262168
  2.5 0.0 copy-start.2
  2.5 0.9 %copy-done.2 = bf16[16,8,1024]{2,1,0:T(8,128)(2,1)S(1)} copy-done((bf16[16,8,1024]{2,1,0:T(8,128)(2,1)S(1)}, bf16[16,8,1024]{2,1,0:T(8,128)(2,1)}, u32[]{:S(2)}) %copy-start.2) | copy-done | bytes 262168
  3.5 0.0 copy-start.3
  3.5 0.9 %copy-done.3 = bf16[16,8,1024]{2,1,0:T(8,128)(2,1)S(1)} copy-done((bf16[16,8,1024]{2,1,0:T(8,128)(2,1)S(1)}, bf16[16,8,1024]{2,1,0:T(8,128)(2,1)}, u32[]{:S(2)}) %copy-start.3) | copy-done | bytes 262168
  4.4 65.0 %shard_map.75 = (bf16[128,1024]{1,0:T(8,128)(2,1)S(1)}, bf16[128,1024]{1,0:T(8,128)(2,1)S(1)}, bf16[128,1024]{1,0:T(8,128)(2,1)S(1)}, bf16[128,1024]{1,0:T(8,128)(2,1)S(1)}) custom-call(bf16[128,1024]{1,0:T(8,128)(2,1)S(1)} %bitcast.12, bf16[128,1024]{1,0:T(8,128)(2,1)S(1)} %bitcast.13, bf16[128,1024]{1,0:T(8,128)(2,1)S(1)} %bitcast.14, ...), custom_call_target="tpu_custom_call" | custom-call | tf_op jit(solution)/shard_map/pallas_call | solution.py:410
  69.5 0.7 copy.12
  70.2 0.7 copy.13
  70.9 0.7 copy.14
  71.6 0.7 copy.15
Async XLA Ops:
  0.6 1.0 %copy-start = (bf16[16,8,1024]{2,1,0:T(8,128)(2,1)S(1)}, bf16[16,8,1024]{2,1,0:T(8,128)(2,1)}, u32[]{:S(2)}) copy-start(bf16[16,8,1024]{2,1,0:T(8,128)(2,1)} %param.4) | copy-start | bytes 786436
  1.6 0.9 %copy-start.1 = (bf16[16,8,1024]{2,1,0:T(8,128)(2,1)S(1)}, bf16[16,8,1024]{2,1,0:T(8,128)(2,1)}, u32[]{:S(2)}) copy-start(bf16[16,8,1024]{2,1,0:T(8,128)(2,1)} %param.5) | copy-start | bytes 786436
  2.5 0.9 %copy-start.2 = (bf16[16,8,1024]{2,1,0:T(8,128)(2,1)S(1)}, bf16[16,8,1024]{2,1,0:T(8,128)(2,1)}, u32[]{:S(2)}) copy-start(bf16[16,8,1024]{2,1,0:T(8,128)(2,1)} %param.6) | copy-start | bytes 786436
  3.5 0.9 %copy-start.3 = (bf16[16,8,1024]{2,1,0:T(8,128)(2,1)S(1)}, bf16[16,8,1024]{2,1,0:T(8,128)(2,1)}, u32[]{:S(2)}) copy-start(bf16[16,8,1024]{2,1,0:T(8,128)(2,1)} %param.7) | copy-start | bytes 786436

commit v3 on v2

v3 whole, which is shorter than its diff:
```python
import functools

import jax
import jax.numpy as jnp
from jax import lax
from jax.experimental import pallas as pl
from jax.experimental.pallas import tpu as pltpu
from jax.sharding import PartitionSpec as P

RADIUS = 6
HEAD = 64
ROWS = 16
COLS = 8
OWN = ROWS * COLS
NN, SS, WW, EE, WC, EC, EXT = 128, 176, 224, 320, 416, 496, 576
SEGMENTS = [
    (0, 8, 0, 0, 128), (128, 8, -6, 0, 48), (176, 8, 16, 0, 48), (224, 6, 0, -6, 96), (320, 6, 0, 8, 96),
    (416, 6, -6, -6, 36), (456, 6, 16, -6, 36), (496, 6, -6, 8, 36), (536, 6, 16, 8, 36),
]
XS = 4
LOG2E = 1.4426950408889634
NEG = -1e30
F32, BF16, I32 = jnp.float32, jnp.bfloat16, jnp.int32
MESH = pl.DeviceIdType.MESH
GREETED = [(1, 0), (-1, 0), (4, 0), (-4, 0), (0, 1), (0, -1)]


def iota(shape, dim):
    return lax.broadcasted_iota(I32, shape, dim)


def div6(x):
    return (x * 171) >> 10


def ext_coords(e):
    row = col = ok = None
    for first, wide, row0, col0, count in SEGMENTS:
        j = jnp.maximum(e - first, 0)
        r = (j >> 3) if wide == 8 else div6(j)
        c = j - wide * r + col0
        r = r + row0
        good = jnp.where(j < count, 1, 0)
        if row is None:
            row, col, ok = r, c, good
        else:
            row = jnp.where(e >= first, r, row)
            col = jnp.where(e >= first, c, col)
            ok = jnp.where(e >= first, good, ok)
    return row, col, ok > 0


def pack_matrix(first_col):
    i = iota((96, OWN), 0)
    r = div6(i)
    src = r * 8 + (i - 6 * r) + first_col
    return jnp.where(iota((96, OWN), 1) == src, 1.0, 0.0).astype(BF16)


def corner_matrix(first_col):
    i = iota((80, 96), 0)
    second = i >= 40
    j = jnp.where(second, i - 40, i)
    r = div6(j)
    src = r * 8 + (j - 6 * r) + first_col + jnp.where(second, 48, 0)
    src = jnp.where(j < 36, src, -1)
    return jnp.where(iota((80, 96), 1) == src, 1.0, 0.0).astype(BF16)


def dot_t(a, b):
    return lax.dot_general(a, b, (((1,), (1,)), ((), ())), preferred_element_type=F32)


def dot(a, b):
    return jnp.dot(a, b, preferred_element_type=F32)


def kernel(n_lat, n_lon, pairs, q_hbm, k_hbm, v_hbm, c_hbm, o_hbm, dq_hbm, dk_hbm, dv_hbm,
           inputs, outputs, ext, snd_side, snd_corner, relay, bias1, bias2, perm, stat_acc, stat_mid, stat_side,
           stat_ext, in_sem, out_sem, side_s, side_r, corner_s, corner_r, strip_s, strip_r, relay_r, pass_s,
           stat_s, stat_r):
    lat, lon = lax.axis_index("lat"), lax.axis_index("lon")
    x = lax.rem(lat, XS)
    heads = 2 * pairs
    half = pairs // 2
    quarter = pairs // 4
    total_rows = n_lat * ROWS
    first = lat * ROWS
    scale = HEAD ** -0.5

    def device(a, b):
        return {"lat": lax.rem(lat + a + n_lat, n_lat), "lon": lax.rem(lon + b + n_lon, n_lon)}

    barrier = pltpu.get_barrier_semaphore()
    for a, b in GREETED:
        pl.semaphore_signal(barrier, inc=1, device_id=device(a, b), device_id_type=MESH)

    loads = [pltpu.make_async_copy(ref, inputs.at[i], in_sem.at[i])
             for i, ref in enumerate((k_hbm, v_hbm, q_hbm, c_hbm))]
    stores = [pltpu.make_async_copy(outputs.at[i], ref, out_sem.at[i])
              for i, ref in enumerate((o_hbm, dq_hbm, dk_hbm, dv_hbm))]
    for load in loads:
        load.start()

    def remote(src, dst, send, recv, to):
        return pltpu.make_async_remote_copy(
            src_ref=src, dst_ref=dst, send_sem=send, recv_sem=recv, device_id=to, device_id_type=MESH)

    def arrays(c):
        return pl.ds(2 * (c // 2), 2)

    def heads_of(c):
        return pl.ds(half * (c % 2), half)

    def from_to(c, d, which):
        at = heads_of(c) if which is None else pl.ds(half * (c % 2) + quarter * which, quarter)
        return (ext.at[arrays(c), at, pl.ds(80 if d == 0 else 0, 48)],
                ext.at[arrays(c), at, pl.ds(NN if d == 0 else SS, 48)])

    def strip(c, d, which=None):
        src, dst = from_to(c, d, which)
        return remote(src, dst, strip_s.at[c, d, 0], strip_r.at[c, d, 0], device(1 if d == 0 else -1, 0))

    def detour(c, d):
        src, _ = from_to(c, d, 1)
        return remote(src, relay.at[c, d], strip_s.at[c, d, 1], relay_r.at[c, d], device(4 if d == 0 else -4, 0))

    def passed(c, d):
        _, dst = from_to(c, d, 1)
        return remote(relay.at[c, d], dst, pass_s.at[c, d], strip_r.at[c, d, 1], device(-3 if d == 0 else 3, 0))

    last = (XS - 1, 0)

    def start_strips(c):
        for d in range(2):
            @pl.when(x != last[d])
            def _():
                strip(c, d).start()

            @pl.when(x == last[d])
            def _():
                detour(c, d).start()
                strip(c, d, 0).start()

    def pass_on(c):
        for d in range(2):
            @pl.when(x == last[d])
            def _():
                detour(c, d).wait_recv()
                passed(c, d).start()

    def wait_strips(c):
        for d in range(2):
            @pl.when(x != last[1 - d])
            def _():
                strip(c, d).wait_recv()

            @pl.when(x == last[1 - d])
            def _():
                strip(c, d, 0).wait_recv()
                passed(c, d).wait_recv()

    def sent_strips(c):
        for d in range(2):
            @pl.when(x != last[d])
            def _():
                strip(c, d).wait_send()

            @pl.when(x == last[d])
            def _():
                strip(c, d, 0).wait_send()
                detour(c, d).wait_send()
                passed(c, d).wait_send()

    def sides(c):
        return [remote(snd_side.at[i, arrays(c), heads_of(c)], ext.at[arrays(c), heads_of(c), pl.ds(to, 96)],
                       side_s.at[c, i], side_r.at[c, i], device(0, b))
                for i, (to, b) in enumerate(((WW, 1), (EE, -1)))]

    def corners(c):
        return [remote(snd_corner.at[i, arrays(c), heads_of(c)], ext.at[arrays(c), heads_of(c), pl.ds(to, 80)],
                       corner_s.at[c, i], corner_r.at[c, i], device(0, b))
                for i, (to, b) in enumerate(((WC, 1), (EC, -1)))]

    def start(copies):
        for copy in copies:
            copy.start()

    def arrived(copies):
        for copy in copies:
            copy.wait_recv()

    def pack(s):
        east, west = pack_matrix(2), pack_matrix(0)
        for a in (2 * s, 2 * s + 1):
            for p in range(pairs):
                block = inputs[a, :, 128 * p:128 * (p + 1)]
                ext[a, p, 0:OWN, :] = block
                snd_side[0, a, p] = dot(east, block).astype(BF16)
                snd_side[1, a, p] = dot(west, block).astype(BF16)

    def send_corners(c):
        wait_strips(c)
        east, west = corner_matrix(2), corner_matrix(0)
        for a in (2 * (c // 2), 2 * (c // 2) + 1):
            for p in range(half * (c % 2), half * (c % 2) + half):
                block = ext[a, p, NN:WW, :]
                snd_corner[0, a, p] = dot(east, block).astype(BF16)
                snd_corner[1, a, p] = dot(west, block).astype(BF16)
        start(corners(c))

    loads[0].wait()
    loads[1].wait()
    pack(0)
    pl.semaphore_wait(barrier, len(GREETED))
    for c in range(2):
        start_strips(c)
        start(sides(c))
    loads[2].wait()
    loads[3].wait()
    pack(1)

    row, col, ok = ext_coords(iota((8, EXT), 1))
    row, col, ok = row[0:1], col[0:1], jnp.where(ok, 1, 0)[0:1]
    token = iota((OWN, EXT), 0)
    near = (jnp.abs(col - (token & 7)) <= RADIUS) & (ok > 0)
    own_row = first + (token >> 3)
    ext_row = first + row
    begin = jnp.clip(own_row - RADIUS, 0, total_rows - 2 * RADIUS - 1)
    inside = near & (ext_row >= begin) & (ext_row <= begin + 2 * RADIUS)
    bias1[...] = jnp.where(inside, 0.0, NEG)
    begin = jnp.clip(ext_row - RADIUS, 0, total_rows - 2 * RADIUS - 1)
    inside = near & (own_row >= begin) & (own_row <= begin + 2 * RADIUS)
    inside = inside & (ext_row >= 0) & (ext_row < total_rows)
    bias2[...] = jnp.where(inside, 0.0, NEG)

    pass_on(0)
    pass_on(1)
    send_corners(0)
    send_corners(1)
    start_strips(2)
    start_strips(3)

    up, down = jnp.where(row < 0, -1, 0), jnp.where(row >= ROWS, 1, 0)
    left, right = jnp.where(col < 0, -3, 0), jnp.where(col >= COLS, 3, 0)
    src = (4 + up + down + left + right) * OWN + (row & (ROWS - 1)) * 8 + (col & (COLS - 1))
    src = jnp.where(ok > 0, src, -1)
    for b in range(9):
        at = iota((OWN, EXT), 0) + b * OWN
        perm[b * OWN:(b + 1) * OWN, :] = jnp.where(at == src, 1.0, 0.0).astype(BF16)

    lane = iota((1, 128), 1)
    lo = jnp.where(lane < HEAD, 1.0, 0.0).astype(BF16)
    hi = jnp.where(lane < HEAD, 0.0, 1.0).astype(BF16)
    lower = iota((OWN, 128), 1) < HEAD

    def by_head(v):
        return jnp.concatenate([v * lo, v * hi], axis=0)

    def merged(v):
        return jnp.where(lower, v[:OWN], v[OWN:])

    def lanes(p):
        return pl.ds(pl.multiple_of(p * 128, 128), 128)

    stat_acc[...] = jnp.zeros_like(stat_acc)

    def forward(p, carry):
        kx, vx = ext[0, p], ext[1, p]
        s = dot_t(by_head(ext[2, p, 0:OWN, :]), kx)
        dw = dot_t(by_head(ext[3, p, 0:OWN, :]), vx)
        acc = stat_acc[...]
        lane_at = iota((OWN, 128), 1)
        rounded, grads = [], []
        for h in range(2):
            of = slice(h * OWN, (h + 1) * OWN)
            t = s[of] * (scale * LOG2E) + bias1[...]
            m = jnp.max(t, axis=1, keepdims=True)
            e = jnp.exp2(t - m)
            total = jnp.sum(e, axis=1, keepdims=True)
            w = e * (1.0 / total)
            rounded.append(w.astype(BF16))
            g = dw[of]
            delta = jnp.sum(w * g, axis=1, keepdims=True)
            grads.append((w * (g - delta)).astype(BF16))
            acc = jnp.where(lane_at == 2 * p + h, m + jnp.log2(total), acc)
            acc = jnp.where(lane_at == heads + 2 * p + h, delta, acc)
        stat_acc[...] = acc
        o = dot(jnp.concatenate(rounded, axis=0), vx)
        dq = dot(jnp.concatenate(grads, axis=0), kx)
        outputs[0, :, lanes(p)] = merged(o).astype(BF16)
        outputs[1, :, lanes(p)] = (merged(dq) * scale).astype(BF16)
        return carry

    def backward(p, carry):
        qx, cx = ext[2, p], ext[3, p]
        s = dot_t(by_head(ext[0, p, 0:OWN, :]), qx)
        dw = dot_t(by_head(ext[1, p, 0:OWN, :]), cx)
        rounded, grads = [], []
        for h in range(2):
            of = slice(h * OWN, (h + 1) * OWN)
            norm = stat_ext[2 * p + h]
            delta = stat_ext[heads + 2 * p + h]
            w = jnp.exp2(s[of] * (scale * LOG2E) + bias2[...] - norm)
            rounded.append(w.astype(BF16))
            grads.append((w * (dw[of] - delta)).astype(BF16))
        dv = dot(jnp.concatenate(rounded, axis=0), cx)
        dk = dot(jnp.concatenate(grads, axis=0), qx)
        outputs[3, :, lanes(p)] = merged(dv).astype(BF16)
        outputs[2, :, lanes(p)] = (merged(dk) * scale).astype(BF16)
        return carry

    arrived(sides(0) + corners(0))
    start(sides(2))
    lax.fori_loop(0, half, forward, 0, unroll=2)
    start(sides(3))
    pass_on(2)
    pass_on(3)
    send_corners(2)
    send_corners(3)
    arrived(sides(1) + corners(1))
    lax.fori_loop(half, pairs, forward, 0, unroll=2)
    stores[0].start()
    stores[1].start()

    stat_mid[1] = stat_acc[...].T[0:2 * heads]
    stats = [remote(stat_mid.at[1], stat_mid.at[i], stat_s.at[k], stat_r.at[k], device(b, 0))
             for k, (i, b) in enumerate(((0, 1), (2, -1)))]
    around = [remote(stat_mid, stat_side.at[k], stat_s.at[2 + k], stat_r.at[2 + k], device(0, b))
              for k, b in enumerate((1, -1))]
    start(stats)
    arrived(stats)
    start(around)
    arrived(sides(2) + corners(2))
    arrived(around)
    whole = jnp.concatenate([stat_side[0, i] for i in range(3)] + [stat_mid[i] for i in range(3)]
                            + [stat_side[1, i] for i in range(3)], axis=1)
    x1 = whole.astype(BF16)
    rest = whole - x1.astype(F32)
    x2 = rest.astype(BF16)
    x3 = (rest - x2.astype(F32)).astype(BF16)
    y = dot(jnp.concatenate([x1, x2, x3], axis=0), perm[...])
    y = (y[0:2 * heads] + y[2 * heads:4 * heads]) + y[4 * heads:6 * heads]
    for i in range(2 * heads):
        stat_ext[i] = y[i:i + 1]

    lax.fori_loop(0, half, backward, 0, unroll=2)
    arrived(sides(3) + corners(3))
    lax.fori_loop(half, pairs, backward, 0, unroll=2)
    stores[2].start()
    stores[3].start()

    for c in range(4):
        sent_strips(c)
        for copy in sides(c) + corners(c):
            copy.wait_send()
    for copy in stats + around:
        copy.wait_send()
    for store in stores:
        store.wait()


def solution(mesh):
    n_lat, n_lon = mesh.shape["lat"], mesh.shape["lon"]

    def shards(queries, keys, values, cotangent):
        width = queries.shape[2]
        pairs = width // 128
        heads = 2 * pairs
        flat = [x.reshape(OWN, width) for x in (queries, keys, values, cotangent)]
        dma = pltpu.SemaphoreType.DMA
        outs = pl.pallas_call(
            functools.partial(kernel, n_lat, n_lon, pairs),
            out_shape=[jax.ShapeDtypeStruct((OWN, width), BF16)] * 4,
            in_specs=[pl.BlockSpec(memory_space=pltpu.HBM)] * 4,
            out_specs=[pl.BlockSpec(memory_space=pltpu.HBM)] * 4,
            scratch_shapes=[
                pltpu.VMEM((4, OWN, width), BF16),
                pltpu.VMEM((4, OWN, width), BF16),
                pltpu.VMEM((4, pairs, EXT, 128), BF16),
                pltpu.VMEM((2, 4, pairs, 96, 128), BF16),
                pltpu.VMEM((2, 4, pairs, 80, 128), BF16),
                pltpu.VMEM((4, 2, 2, pairs // 4, 48, 128), BF16),
                pltpu.VMEM((OWN, EXT), F32),
                pltpu.VMEM((OWN, EXT), F32),
                pltpu.VMEM((9 * OWN, EXT), BF16),
                pltpu.VMEM((OWN, 128), F32),
                pltpu.VMEM((3, 2 * heads, OWN), F32),
                pltpu.VMEM((2, 3, 2 * heads, OWN), F32),
                pltpu.VMEM((2 * heads, 1, EXT), F32),
                dma((4,)), dma((4,)), dma((4, 2)), dma((4, 2)), dma((4, 2)), dma((4, 2)),
                dma((4, 2, 2)), dma((4, 2, 2)), dma((4, 2)), dma((4, 2)), dma((4,)), dma((4,)),
            ],
            compiler_params=pltpu.CompilerParams(
                collective_id=0, has_side_effects=True, vmem_limit_bytes=63 * 1024 * 1024),
        )(*flat)
        return tuple(x.reshape(ROWS, COLS, width) for x in outs)

    spec = P("lat", "lon", None)
    return jax.shard_map(shards, mesh=mesh, in_specs=(spec,) * 4, out_specs=(spec,) * 4, check_vma=False)
```

time: 72.5 us -> 64 us (0.88)
  the two profiles are of different devices: /device:TPU:1 before, /device:TPU:8 now
where the time goes in v3:
time: 64 us; the launch traced here: 63.8 us
  Pallas kernels  58.7 us (92%)
  local copies, waits for them, and re-layouts  4.5 us (7%)
  between operations  0.65 us (1%)
    pallas_call x1, Pallas kernels, shards(): pl.pallas_call(functools.partial(kernel, n_lat, n_lon, pairs), out_shape=...  58.7 us
    unnamed x10, local copies, waits for them, and re-layouts  4.5 us

profile of v3, /device:TPU:8, one launch (start us, length us, event | category | flops | bytes accessed | tf_op | source)
XLA Modules:
  0.0 63.8 jit_solution(10853468831166417911)
XLA Ops:
  0.6 58.7 %shard_map.75 = (bf16[128,1024]{1,0:T(8,128)(2,1)}, bf16[128,1024]{1,0:T(8,128)(2,1)}, bf16[128,1024]{1,0:T(8,128)(2,1)}, bf16[128,1024]{1,0:T(8,128)(2,1)}) custom-call(bf16[128,1024]{1,0:T(8,128)(2,1)} %bitcast.12, bf16[128,1024]{1,0:T(8,128)(2,1)} %bitcast.13, bf16[128,1024]{1,0:T(8,128)(2,1)} %bitcast.14, bf16[128,1024]{1,0:T(8,128)(2,1)} %bitcast.15), custom_call_target="tpu_custom_call" | custom-call | tf_op jit(solution)/shard_map/pallas_call | solution.py:372
  59.3 0.0 copy-start.2
  59.3 1.7 %copy.12 = bf16[16,8,1024]{2,1,0:T(8,128)(2,1)} copy(bf16[16,8,1024]{2,1,0:T(8,128)(2,1)} %bitcast.11) | data formatting | bytes 524288
  61.0 0.0 copy-done.2
  61.0 0.0 copy-start.1
  61.0 0.7 %copy.13 = bf16[16,8,1024]{2,1,0:T(8,128)(2,1)} copy(bf16[16,8,1024]{2,1,0:T(8,128)(2,1)S(1)} %bitcast.10) | data formatting | bytes 524288
  61.7 0.3 copy-done.1
  62.1 0.0 copy-start
  62.1 0.7 %copy.14 = bf16[16,8,1024]{2,1,0:T(8,128)(2,1)} copy(bf16[16,8,1024]{2,1,0:T(8,128)(2,1)S(1)} %bitcast.9) | data formatting | bytes 524288
  62.8 0.3 copy-done
  63.1 0.7 %copy.15 = bf16[16,8,1024]{2,1,0:T(8,128)(2,1)} copy(bf16[16,8,1024]{2,1,0:T(8,128)(2,1)S(1)} %bitcast.8) | data formatting | bytes 524288
Async XLA Ops:
  59.3 1.7 %copy-start.2 = (bf16[128,1024]{1,0:T(8,128)(2,1)S(1)}, bf16[128,1024]{1,0:T(8,128)(2,1)}, u32[]{:S(2)}) copy-start(bf16[128,1024]{1,0:T(8,128)(2,1)} %get-tuple-element.9) | copy-start | bytes 786436
  61.0 1.0 %copy-start.1 = (bf16[128,1024]{1,0:T(8,128)(2,1)S(1)}, bf16[128,1024]{1,0:T(8,128)(2,1)}, u32[]{:S(2)}) copy-start(bf16[128,1024]{1,0:T(8,128)(2,1)} %get-tuple-element.10) | copy-start | bytes 786436
  62.1 1.0 %copy-start = (bf16[128,1024]{1,0:T(8,128)(2,1)S(1)}, bf16[128,1024]{1,0:T(8,128)(2,1)}, u32[]{:S(2)}) copy-start(bf16[128,1024]{1,0:T(8,128)(2,1)} %get-tuple-element.11) | copy-start | bytes 786436

commit v4 on v3

--- a/solution.py
+++ b/solution.py
@@ -22,7 +22,8 @@
 NEG = -1e30
 F32, BF16, I32 = jnp.float32, jnp.bfloat16, jnp.int32
 MESH = pl.DeviceIdType.MESH
-GREETED = [(1, 0), (-1, 0), (4, 0), (-4, 0), (0, 1), (0, -1)]
+GREETED = [(1, 0), (-1, 0), (4, 0), (-4, 0), (3, 0), (-3, 0), (0, 1), (0, -1)]
+AROUND = [(a, b) for a in (-1, 0, 1) for b in (-1, 0, 1) if (a, b) != (0, 0)]
 
 
 def iota(shape, dim):
@@ -76,7 +77,7 @@
 
 
 def kernel(n_lat, n_lon, pairs, q_hbm, k_hbm, v_hbm, c_hbm, o_hbm, dq_hbm, dk_hbm, dv_hbm,
-           inputs, outputs, ext, snd_side, snd_corner, relay, bias1, bias2, perm, stat_acc, stat_mid, stat_side,
+           inputs, outputs, ext, snd_side, snd_corner, relay, bias1, bias2, perm, stat_acc, stat_own, stat_in,
            stat_ext, in_sem, out_sem, side_s, side_r, corner_s, corner_r, strip_s, strip_r, relay_r, pass_s,
            stat_s, stat_r):
     lat, lon = lax.axis_index("lat"), lax.axis_index("lon")
@@ -123,11 +124,11 @@
 
     def detour(c, d):
         src, _ = from_to(c, d, 1)
-        return remote(src, relay.at[c, d], strip_s.at[c, d, 1], relay_r.at[c, d], device(4 if d == 0 else -4, 0))
+        return remote(src, relay.at[c, d], strip_s.at[c, d, 1], relay_r.at[c, d], device(-3 if d == 0 else 3, 0))
 
     def passed(c, d):
         _, dst = from_to(c, d, 1)
-        return remote(relay.at[c, d], dst, pass_s.at[c, d], strip_r.at[c, d, 1], device(-3 if d == 0 else 3, 0))
+        return remote(relay.at[c, d], dst, pass_s.at[c, d], strip_r.at[c, d, 1], device(4 if d == 0 else -4, 0))
 
     last = (XS - 1, 0)
 
@@ -139,12 +140,11 @@
 
             @pl.when(x == last[d])
             def _():
-                detour(c, d).start()
                 strip(c, d, 0).start()
 
     def pass_on(c):
         for d in range(2):
-            @pl.when(x == last[d])
+            @pl.when(x == last[1 - d])
             def _():
                 detour(c, d).wait_recv()
                 passed(c, d).start()
@@ -170,6 +170,9 @@
             def _():
                 strip(c, d, 0).wait_send()
                 detour(c, d).wait_send()
+
+            @pl.when(x == last[1 - d])
+            def _():
                 passed(c, d).wait_send()
 
     def sides(c):
@@ -209,16 +212,20 @@
                 snd_corner[1, a, p] = dot(west, block).astype(BF16)
         start(corners(c))
 
-    loads[0].wait()
-    loads[1].wait()
+    for load in loads:
+        load.wait()
     pack(0)
+    pack(1)
     pl.semaphore_wait(barrier, len(GREETED))
-    for c in range(2):
+    for d in range(2):
+        @pl.when(x == last[d])
+        def _():
+            for c in range(4):
+                detour(c, d).start()
+    for c in range(4):
         start_strips(c)
-        start(sides(c))
-    loads[2].wait()
-    loads[3].wait()
-    pack(1)
+        if c < 3:
+            start(sides(c))
 
     row, col, ok = ext_coords(iota((8, EXT), 1))
     row, col, ok = row[0:1], col[0:1], jnp.where(ok, 1, 0)[0:1]
@@ -234,21 +241,20 @@
     inside = inside & (ext_row >= 0) & (ext_row < total_rows)
     bias2[...] = jnp.where(inside, 0.0, NEG)
 
-    pass_on(0)
-    pass_on(1)
-    send_corners(0)
-    send_corners(1)
-    start_strips(2)
-    start_strips(3)
-
-    up, down = jnp.where(row < 0, -1, 0), jnp.where(row >= ROWS, 1, 0)
-    left, right = jnp.where(col < 0, -3, 0), jnp.where(col >= COLS, 3, 0)
+    up, down = jnp.where(row < 0, -3, 0), jnp.where(row >= ROWS, 3, 0)
+    left, right = jnp.where(col < 0, -1, 0), jnp.where(col >= COLS, 1, 0)
     src = (4 + up + down + left + right) * OWN + (row & (ROWS - 1)) * 8 + (col & (COLS - 1))
     src = jnp.where(ok > 0, src, -1)
     for b in range(9):
         at = iota((OWN, EXT), 0) + b * OWN
         perm[b * OWN:(b + 1) * OWN, :] = jnp.where(at == src, 1.0, 0.0).astype(BF16)
 
+    for c in range(4):
+        pass_on(c)
+    send_corners(0)
+    send_corners(1)
+    start(sides(3))
+
     lane = iota((1, 128), 1)
     lo = jnp.where(lane < HEAD, 1.0, 0.0).astype(BF16)
     hi = jnp.where(lane < HEAD, 0.0, 1.0).astype(BF16)
@@ -263,12 +269,11 @@
     def lanes(p):
         return pl.ds(pl.multiple_of(p * 128, 128), 128)
 
-    stat_acc[...] = jnp.zeros_like(stat_acc)
-
     def forward(p, carry):
         kx, vx = ext[0, p], ext[1, p]
         s = dot_t(by_head(ext[2, p, 0:OWN, :]), kx)
         dw = dot_t(by_head(ext[3, p, 0:OWN, :]), vx)
+        at = 2 * lax.rem(p, half)
         acc = stat_acc[...]
         lane_at = iota((OWN, 128), 1)
         rounded, grads = [], []
@@ -283,8 +288,8 @@
             g = dw[of]
             delta = jnp.sum(w * g, axis=1, keepdims=True)
             grads.append((w * (g - delta)).astype(BF16))
-            acc = jnp.where(lane_at == 2 * p + h, m + jnp.log2(total), acc)
-            acc = jnp.where(lane_at == heads + 2 * p + h, delta, acc)
+            acc = jnp.where(lane_at == at + h, m + jnp.log2(total), acc)
+            acc = jnp.where(lane_at == pairs + at + h, delta, acc)
         stat_acc[...] = acc
         o = dot(jnp.concatenate(rounded, axis=0), vx)
         dq = dot(jnp.concatenate(grads, axis=0), kx)
@@ -310,41 +315,43 @@
         outputs[2, :, lanes(p)] = (merged(dk) * scale).astype(BF16)
         return carry
 
+    def stats(i):
+        return [remote(stat_own.at[i], stat_in.at[i, n], stat_s.at[i, n], stat_r.at[i, n], device(-a, -b))
+                for n, (a, b) in enumerate(AROUND)]
+
+    def send_stats(i):
+        stat_own[i] = stat_acc[...].T[0:heads]
+        start(stats(i))
+
+    def spread_stats(i):
+        arrived(stats(i))
+        whole = jnp.concatenate([stat_in[i, n] for n in range(4)] + [stat_own[i]]
+                                + [stat_in[i, n] for n in range(4, 8)], axis=1)
+        x1 = whole.astype(BF16)
+        rest = whole - x1.astype(F32)
+        x2 = rest.astype(BF16)
+        x3 = (rest - x2.astype(F32)).astype(BF16)
+        y = dot(jnp.concatenate([x1, x2, x3], axis=0), perm[...])
+        y = (y[0:heads] + y[heads:2 * heads]) + y[2 * heads:3 * heads]
+        for k in range(pairs):
+            stat_ext[pairs * i + k] = y[k:k + 1]
+            stat_ext[heads + pairs * i + k] = y[pairs + k:pairs + k + 1]
+
+    stat_acc[...] = jnp.zeros_like(stat_acc)
     arrived(sides(0) + corners(0))
-    start(sides(2))
+    send_corners(2)
     lax.fori_loop(0, half, forward, 0, unroll=2)
-    start(sides(3))
-    pass_on(2)
-    pass_on(3)
-    send_corners(2)
+    send_stats(0)
     send_corners(3)
     arrived(sides(1) + corners(1))
     lax.fori_loop(half, pairs, forward, 0, unroll=2)
+    send_stats(1)
     stores[0].start()
     stores[1].start()
-
-    stat_mid[1] = stat_acc[...].T[0:2 * heads]
-    stats = [remote(stat_mid.at[1], stat_mid.at[i], stat_s.at[k], stat_r.at[k], device(b, 0))
-             for k, (i, b) in enumerate(((0, 1), (2, -1)))]
-    around = [remote(stat_mid, stat_side.at[k], stat_s.at[2 + k], stat_r.at[2 + k], device(0, b))
-              for k, b in enumerate((1, -1))]
-    start(stats)
-    arrived(stats)
-    start(around)
+    spread_stats(0)
     arrived(sides(2) + corners(2))
-    arrived(around)
-    whole = jnp.concatenate([stat_side[0, i] for i in range(3)] + [stat_mid[i] for i in range(3)]
-                            + [stat_side[1, i] for i in range(3)], axis=1)
-    x1 = whole.astype(BF16)
-    rest = whole - x1.astype(F32)
-    x2 = rest.astype(BF16)
-    x3 = (rest - x2.astype(F32)).astype(BF16)
-    y = dot(jnp.concatenate([x1, x2, x3], axis=0), perm[...])
-    y = (y[0:2 * heads] + y[2 * heads:4 * heads]) + y[4 * heads:6 * heads]
-    for i in range(2 * heads):
-        stat_ext[i] = y[i:i + 1]
-
     lax.fori_loop(0, half, backward, 0, unroll=2)
+    spread_stats(1)
     arrived(sides(3) + corners(3))
     lax.fori_loop(half, pairs, backward, 0, unroll=2)
     stores[2].start()
@@ -354,8 +361,9 @@
         sent_strips(c)
         for copy in sides(c) + corners(c):
             copy.wait_send()
-    for copy in stats + around:
-        copy.wait_send()
+    for i in range(2):
+        for copy in stats(i):
+            copy.wait_send()
     for store in stores:
         store.wait()
 
@@ -385,11 +393,11 @@
                 pltpu.VMEM((OWN, EXT), F32),
                 pltpu.VMEM((9 * OWN, EXT), BF16),
                 pltpu.VMEM((OWN, 128), F32),
-                pltpu.VMEM((3, 2 * heads, OWN), F32),
-                pltpu.VMEM((2, 3, 2 * heads, OWN), F32),
+                pltpu.VMEM((2, heads, OWN), F32),
+                pltpu.VMEM((2, 8, heads, OWN), F32),
                 pltpu.VMEM((2 * heads, 1, EXT), F32),
                 dma((4,)), dma((4,)), dma((4, 2)), dma((4, 2)), dma((4, 2)), dma((4, 2)),
-                dma((4, 2, 2)), dma((4, 2, 2)), dma((4, 2)), dma((4, 2)), dma((4,)), dma((4,)),
+                dma((4, 2, 2)), dma((4, 2, 2)), dma((4, 2)), dma((4, 2)), dma((2, 8)), dma((2, 8)),
             ],
             compiler_params=pltpu.CompilerParams(
                 collective_id=0, has_side_effects=True, vmem_limit_bytes=63 * 1024 * 1024),

time: 64 us -> 56.8 us (0.89)
  the two profiles are of different devices: /device:TPU:8 before, /device:TPU:1 now
where the time goes in v4:
time: 56.8 us; the launch traced here: 56.6 us
  Pallas kernels  51.5 us (91%)
  local copies, waits for them, and re-layouts  4.5 us (8%)
  between operations  0.65 us (1%)
    pallas_call x1, Pallas kernels, shards(): pl.pallas_call(functools.partial(kernel, n_lat, n_lon, pairs), out_shape=...  51.5 us
    unnamed x10, local copies, waits for them, and re-layouts  4.5 us

profile of v4, /device:TPU:1, one launch (start us, length us, event | category | flops | bytes accessed | tf_op | source)
XLA Modules:
  0.0 56.6 jit_solution(5849087681243563221)
XLA Ops:
  0.6 51.5 %shard_map.75 = (bf16[128,1024]{1,0:T(8,128)(2,1)}, bf16[128,1024]{1,0:T(8,128)(2,1)}, bf16[128,1024]{1,0:T(8,128)(2,1)}, bf16[128,1024]{1,0:T(8,128)(2,1)}) custom-call(bf16[128,1024]{1,0:T(8,128)(2,1)} %bitcast.12, bf16[128,1024]{1,0:T(8,128)(2,1)} %bitcast.13, bf16[128,1024]{1,0:T(8,128)(2,1)} %bitcast.14, bf16[128,1024]{1,0:T(8,128)(2,1)} %bitcast.15), custom_call_target="tpu_custom_call" | custom-call | tf_op jit(solution)/shard_map/pallas_call | solution.py:380
  52.1 0.0 copy-start.2
  52.1 1.7 %copy.12 = bf16[16,8,1024]{2,1,0:T(8,128)(2,1)} copy(bf16[16,8,1024]{2,1,0:T(8,128)(2,1)} %bitcast.11) | data formatting | bytes 524288
  53.8 0.0 copy-done.2
  53.8 0.0 copy-start.1
  53.8 0.7 %copy.13 = bf16[16,8,1024]{2,1,0:T(8,128)(2,1)} copy(bf16[16,8,1024]{2,1,0:T(8,128)(2,1)S(1)} %bitcast.10) | data formatting | bytes 524288
  54.5 0.3 copy-done.1
  54.9 0.0 copy-start
  54.9 0.7 %copy.14 = bf16[16,8,1024]{2,1,0:T(8,128)(2,1)} copy(bf16[16,8,1024]{2,1,0:T(8,128)(2,1)S(1)} %bitcast.9) | data formatting | bytes 524288
  55.6 0.3 copy-done
  55.9 0.7 %copy.15 = bf16[16,8,1024]{2,1,0:T(8,128)(2,1)} copy(bf16[16,8,1024]{2,1,0:T(8,128)(2,1)S(1)} %bitcast.8) | data formatting | bytes 524288
Async XLA Ops:
  52.1 1.7 %copy-start.2 = (bf16[128,1024]{1,0:T(8,128)(2,1)S(1)}, bf16[128,1024]{1,0:T(8,128)(2,1)}, u32[]{:S(2)}) copy-start(bf16[128,1024]{1,0:T(8,128)(2,1)} %get-tuple-element.9) | copy-start | bytes 786436
  53.8 1.0 %copy-start.1 = (bf16[128,1024]{1,0:T(8,128)(2,1)S(1)}, bf16[128,1024]{1,0:T(8,128)(2,1)}, u32[]{:S(2)}) copy-start(bf16[128,1024]{1,0:T(8,128)(2,1)} %get-tuple-element.10) | copy-start | bytes 786436
  54.9 1.0 %copy-start = (bf16[128,1024]{1,0:T(8,128)(2,1)S(1)}, bf16[128,1024]{1,0:T(8,128)(2,1)}, u32[]{:S(2)}) copy-start(bf16[128,1024]{1,0:T(8,128)(2,1)} %get-tuple-element.11) | copy-start | bytes 786436

commit v5 on v4

--- a/solution.py
+++ b/solution.py
@@ -12,17 +12,18 @@
 ROWS = 16
 COLS = 8
 OWN = ROWS * COLS
-NN, SS, WW, EE, WC, EC, EXT = 128, 176, 224, 320, 416, 496, 576
+NN, SS, WW, EE, WC, EC, EXT = 128, 176, 224, 320, 416, 512, 608
 SEGMENTS = [
     (0, 8, 0, 0, 128), (128, 8, -6, 0, 48), (176, 8, 16, 0, 48), (224, 6, 0, -6, 96), (320, 6, 0, 8, 96),
-    (416, 6, -6, -6, 36), (456, 6, 16, -6, 36), (496, 6, -6, 8, 36), (536, 6, 16, 8, 36),
+    (416, 6, -8, -6, 48), (464, 6, 16, -6, 48), (512, 6, -8, 8, 48), (560, 6, 16, 8, 48),
 ]
 XS = 4
 LOG2E = 1.4426950408889634
 NEG = -1e30
 F32, BF16, I32 = jnp.float32, jnp.bfloat16, jnp.int32
 MESH = pl.DeviceIdType.MESH
-GREETED = [(1, 0), (-1, 0), (4, 0), (-4, 0), (3, 0), (-3, 0), (0, 1), (0, -1)]
+GREETED = [(a, 0) for a in (-4, -3, -2, -1, 1, 2, 3, 4)] + [(0, 1), (0, -1)]
+FOUR, TWO = [(0, 0, 1), (1, 1, 1), (2, 2, 1), (3, 3, 1)], [(0, 0, 2), (3, 2, 2)]
 AROUND = [(a, b) for a in (-1, 0, 1) for b in (-1, 0, 1) if (a, b) != (0, 0)]
 
 
@@ -59,13 +60,11 @@
 
 
 def corner_matrix(first_col):
-    i = iota((80, 96), 0)
-    second = i >= 40
-    j = jnp.where(second, i - 40, i)
-    r = div6(j)
-    src = r * 8 + (j - 6 * r) + first_col + jnp.where(second, 48, 0)
-    src = jnp.where(j < 36, src, -1)
-    return jnp.where(iota((80, 96), 1) == src, 1.0, 0.0).astype(BF16)
+    i = iota((96, 96), 0)
+    r = div6(i)
+    src = (r - 2) * 8 + (i - 6 * r) + first_col
+    src = jnp.where((i >= 12) & (i < 84), src, -1)
+    return jnp.where(iota((96, 96), 1) == src, 1.0, 0.0).astype(BF16)
 
 
 def dot_t(a, b):
@@ -78,13 +77,13 @@
 
 def kernel(n_lat, n_lon, pairs, q_hbm, k_hbm, v_hbm, c_hbm, o_hbm, dq_hbm, dk_hbm, dv_hbm,
            inputs, outputs, ext, snd_side, snd_corner, relay, bias1, bias2, perm, stat_acc, stat_own, stat_in,
-           stat_ext, in_sem, out_sem, side_s, side_r, corner_s, corner_r, strip_s, strip_r, relay_r, pass_s,
+           stat_ext, in_sem, out_sem, side_s, side_r, corner_s, corner_r, cut_s, strip_s, strip_r, relay_r, pass_s,
            stat_s, stat_r):
     lat, lon = lax.axis_index("lat"), lax.axis_index("lon")
     x = lax.rem(lat, XS)
     heads = 2 * pairs
     half = pairs // 2
-    quarter = pairs // 4
+    ring = min(16, n_lon)
     total_rows = n_lat * ROWS
     first = lat * ROWS
     scale = HEAD ** -0.5
@@ -113,24 +112,41 @@
     def heads_of(c):
         return pl.ds(half * (c % 2), half)
 
-    def from_to(c, d, which):
-        at = heads_of(c) if which is None else pl.ds(half * (c % 2) + quarter * which, quarter)
+    def from_to(c, d, lo, n):
+        at = pl.ds(half * (c % 2) + lo, n)
         return (ext.at[arrays(c), at, pl.ds(80 if d == 0 else 0, 48)],
                 ext.at[arrays(c), at, pl.ds(NN if d == 0 else SS, 48)])
 
-    def strip(c, d, which=None):
-        src, dst = from_to(c, d, which)
+    last = (XS - 1, 0)
+    edge = lax.rem(lon, ring)
+    at_wrap = (edge < 2) | (edge >= ring - 2)
+    plans = [(FOUR, at_wrap), (TWO, jnp.logical_not(at_wrap))]
+
+    def strip(c, d):
+        src, dst = from_to(c, d, 0, half)
         return remote(src, dst, strip_s.at[c, d, 0], strip_r.at[c, d, 0], device(1 if d == 0 else -1, 0))
 
-    def detour(c, d):
-        src, _ = from_to(c, d, 1)
-        return remote(src, relay.at[c, d], strip_s.at[c, d, 1], relay_r.at[c, d], device(-3 if d == 0 else 3, 0))
-
-    def passed(c, d):
-        _, dst = from_to(c, d, 1)
-        return remote(relay.at[c, d], dst, pass_s.at[c, d], strip_r.at[c, d, 1], device(4 if d == 0 else -4, 0))
-
-    last = (XS - 1, 0)
+    def part(c, d, j, lo, n):
+        src, dst = from_to(c, d, lo, n)
+        if j == last[d]:
+            return remote(src, dst, strip_s.at[c, d, j], strip_r.at[c, d, j], device(1 if d == 0 else -1, 0))
+        return remote(src, relay.at[c, d, :, pl.ds(0, n)], strip_s.at[c, d, j], relay_r.at[c, d],
+                      device(j - XS + 1 if d == 0 else j, 0))
+
+    def passed(c, d, j, lo, n):
+        _, dst = from_to(c, d, lo, n)
+        return remote(relay.at[c, d, :, pl.ds(0, n)], dst, pass_s.at[c, d], strip_r.at[c, d, j],
+                      device(XS - j if d == 0 else -1 - j, 0))
+
+    def start_detours():
+        for plan, here in plans:
+            for d in range(2):
+                @pl.when(here & (x == last[d]))
+                def _():
+                    for c in range(4):
+                        for j, lo, n in plan:
+                            if j != last[d]:
+                                part(c, d, j, lo, n).start()
 
     def start_strips(c):
         for d in range(2):
@@ -138,16 +154,22 @@
             def _():
                 strip(c, d).start()
 
-            @pl.when(x == last[d])
-            def _():
-                strip(c, d, 0).start()
+            for plan, here in plans:
+                @pl.when(here & (x == last[d]))
+                def _():
+                    for j, lo, n in plan:
+                        if j == last[d]:
+                            part(c, d, j, lo, n).start()
 
     def pass_on(c):
-        for d in range(2):
-            @pl.when(x == last[1 - d])
-            def _():
-                detour(c, d).wait_recv()
-                passed(c, d).start()
+        for plan, here in plans:
+            for d in range(2):
+                for j, lo, n in plan:
+                    if j != last[d]:
+                        @pl.when(here & (x == j))
+                        def _():
+                            part(c, d, j, lo, n).wait_recv()
+                            passed(c, d, j, lo, n).start()
 
     def wait_strips(c):
         for d in range(2):
@@ -155,10 +177,11 @@
             def _():
                 strip(c, d).wait_recv()
 
-            @pl.when(x == last[1 - d])
-            def _():
-                strip(c, d, 0).wait_recv()
-                passed(c, d).wait_recv()
+            for plan, here in plans:
+                @pl.when(here & (x == last[1 - d]))
+                def _():
+                    for j, lo, n in plan:
+                        passed(c, d, j, lo, n).wait_recv()
 
     def sent_strips(c):
         for d in range(2):
@@ -166,24 +189,54 @@
             def _():
                 strip(c, d).wait_send()
 
-            @pl.when(x == last[d])
-            def _():
-                strip(c, d, 0).wait_send()
-                detour(c, d).wait_send()
-
-            @pl.when(x == last[1 - d])
-            def _():
-                passed(c, d).wait_send()
+            for plan, here in plans:
+                @pl.when(here & (x == last[d]))
+                def _():
+                    for j, lo, n in plan:
+                        part(c, d, j, lo, n).wait_send()
+
+                for j, lo, n in plan:
+                    if j != last[d]:
+                        @pl.when(here & (x == j))
+                        def _():
+                            passed(c, d, j, lo, n).wait_send()
 
     def sides(c):
         return [remote(snd_side.at[i, arrays(c), heads_of(c)], ext.at[arrays(c), heads_of(c), pl.ds(to, 96)],
                        side_s.at[c, i], side_r.at[c, i], device(0, b))
                 for i, (to, b) in enumerate(((WW, 1), (EE, -1)))]
 
-    def corners(c):
-        return [remote(snd_corner.at[i, arrays(c), heads_of(c)], ext.at[arrays(c), heads_of(c), pl.ds(to, 80)],
-                       corner_s.at[c, i], corner_r.at[c, i], device(0, b))
-                for i, (to, b) in enumerate(((WC, 1), (EC, -1)))]
+    wraps = (edge == 0, edge == ring - 1)
+    poles = (x == 0, x == XS - 1)
+
+    def corner(c, i, k):
+        at = (arrays(c), heads_of(c))
+        return remote(snd_corner.at[i, *at, pl.ds(48 * k, 48)], ext.at[*at, pl.ds((WC, EC)[i] + 48 * k, 48)],
+                      corner_s.at[c, i, k], corner_r.at[c, i, k], device(0, 1 - 2 * i))
+
+    def cut(c, i, k):
+        at = (arrays(c), heads_of(c))
+        return remote(ext.at[*at, pl.ds((WW, EE)[i] + 48 * (1 - k), 48)], ext.at[*at, pl.ds((WC, EC)[i] + 48 * k, 48)],
+                      cut_s.at[c, i, k], corner_r.at[c, i, k], device(1 - 2 * k, 0))
+
+    def each_corner(c, do):
+        for i in range(2):
+            for k in range(2):
+                @pl.when(jnp.logical_not(wraps[1 - i]) | poles[k])
+                def _():
+                    do(corner(c, i, k))
+
+    def each_cut(c, do):
+        for i in range(2):
+            for k in range(2):
+                @pl.when(wraps[i] & jnp.logical_not(poles[1 - k]))
+                def _():
+                    do(cut(c, i, k))
+
+    def wait_corners(c):
+        for i in range(2):
+            for k in range(2):
+                corner(c, i, k).wait_recv()
 
     def start(copies):
         for copy in copies:
@@ -210,23 +263,21 @@
                 block = ext[a, p, NN:WW, :]
                 snd_corner[0, a, p] = dot(east, block).astype(BF16)
                 snd_corner[1, a, p] = dot(west, block).astype(BF16)
-        start(corners(c))
+        each_corner(c, lambda copy: copy.start())
+
+    def land_sides(c):
+        arrived(sides(c))
+        each_cut(c, lambda copy: copy.start())
 
     for load in loads:
         load.wait()
     pack(0)
     pack(1)
     pl.semaphore_wait(barrier, len(GREETED))
-    for d in range(2):
-        @pl.when(x == last[d])
-        def _():
-            for c in range(4):
-                detour(c, d).start()
-    for c in range(4):
-        start_strips(c)
-        if c < 3:
-            start(sides(c))
-
+    start_detours()
+    start_strips(0)
+    start_strips(1)
+    start(sides(0))
     row, col, ok = ext_coords(iota((8, EXT), 1))
     row, col, ok = row[0:1], col[0:1], jnp.where(ok, 1, 0)[0:1]
     token = iota((OWN, EXT), 0)
@@ -249,12 +300,21 @@
         at = iota((OWN, EXT), 0) + b * OWN
         perm[b * OWN:(b + 1) * OWN, :] = jnp.where(at == src, 1.0, 0.0).astype(BF16)
 
-    for c in range(4):
-        pass_on(c)
+    pass_on(0)
+    pass_on(1)
+    start(sides(1))
+    start_strips(2)
+    start_strips(3)
+    pass_on(2)
+    pass_on(3)
+    start(sides(2))
     send_corners(0)
     send_corners(1)
     start(sides(3))
-
+    land_sides(0)
+    land_sides(1)
+    land_sides(2)
+    send_corners(2)
     lane = iota((1, 128), 1)
     lo = jnp.where(lane < HEAD, 1.0, 0.0).astype(BF16)
     hi = jnp.where(lane < HEAD, 0.0, 1.0).astype(BF16)
@@ -338,28 +398,30 @@
             stat_ext[heads + pairs * i + k] = y[pairs + k:pairs + k + 1]
 
     stat_acc[...] = jnp.zeros_like(stat_acc)
-    arrived(sides(0) + corners(0))
-    send_corners(2)
-    lax.fori_loop(0, half, forward, 0, unroll=2)
+    wait_corners(0)
+    lax.fori_loop(0, half, forward, 0, unroll=4)
     send_stats(0)
+    land_sides(3)
     send_corners(3)
-    arrived(sides(1) + corners(1))
-    lax.fori_loop(half, pairs, forward, 0, unroll=2)
+    wait_corners(1)
+    lax.fori_loop(half, pairs, forward, 0, unroll=4)
     send_stats(1)
     stores[0].start()
     stores[1].start()
     spread_stats(0)
-    arrived(sides(2) + corners(2))
-    lax.fori_loop(0, half, backward, 0, unroll=2)
+    wait_corners(2)
+    lax.fori_loop(0, half, backward, 0, unroll=4)
     spread_stats(1)
-    arrived(sides(3) + corners(3))
-    lax.fori_loop(half, pairs, backward, 0, unroll=2)
+    wait_corners(3)
+    lax.fori_loop(half, pairs, backward, 0, unroll=4)
     stores[2].start()
     stores[3].start()
 
     for c in range(4):
         sent_strips(c)
-        for copy in sides(c) + corners(c):
+        each_corner(c, lambda copy: copy.wait_send())
+        each_cut(c, lambda copy: copy.wait_send())
+        for copy in sides(c):
             copy.wait_send()
     for i in range(2):
         for copy in stats(i):
@@ -387,8 +449,8 @@
                 pltpu.VMEM((4, OWN, width), BF16),
                 pltpu.VMEM((4, pairs, EXT, 128), BF16),
                 pltpu.VMEM((2, 4, pairs, 96, 128), BF16),
-                pltpu.VMEM((2, 4, pairs, 80, 128), BF16),
-                pltpu.VMEM((4, 2, 2, pairs // 4, 48, 128), BF16),
+                pltpu.VMEM((2, 4, pairs, 96, 128), BF16),
+                pltpu.VMEM((4, 2, 2, 2, 48, 128), BF16),
                 pltpu.VMEM((OWN, EXT), F32),
                 pltpu.VMEM((OWN, EXT), F32),
                 pltpu.VMEM((9 * OWN, EXT), BF16),
@@ -396,8 +458,8 @@
                 pltpu.VMEM((2, heads, OWN), F32),
                 pltpu.VMEM((2, 8, heads, OWN), F32),
                 pltpu.VMEM((2 * heads, 1, EXT), F32),
-                dma((4,)), dma((4,)), dma((4, 2)), dma((4, 2)), dma((4, 2)), dma((4, 2)),
-                dma((4, 2, 2)), dma((4, 2, 2)), dma((4, 2)), dma((4, 2)), dma((2, 8)), dma((2, 8)),
+                dma((4,)), dma((4,)), dma((4, 2)), dma((4, 2)), dma((4, 2, 2)), dma((4, 2, 2)), dma((4, 2, 2)),
+                dma((4, 2, XS)), dma((4, 2, XS)), dma((4, 2)), dma((4, 2)), dma((2, 8)), dma((2, 8)),
             ],
             compiler_params=pltpu.CompilerParams(
                 collective_id=0, has_side_effects=True, vmem_limit_bytes=63 * 1024 * 1024),

time: 56.8 us -> 51 us (0.90)
  Pallas kernels: 51.5 us -> 45.7 us
    pallas_call x1, Pallas kernels: 51.5 us -> 45.7 us  [shards(): pl.pallas_call(functools.partial(kernel, n_lat, n_lon, pairs), out_shape=...]
where the time goes in v5:
time: 51 us; the launch traced here: 50.8 us
  Pallas kernels  45.7 us (90%)
  local copies, waits for them, and re-layouts  4.5 us (9%)
  between operations  0.65 us (1%)
    pallas_call x1, Pallas kernels, shards(): pl.pallas_call(functools.partial(kernel, n_lat, n_lon, pairs), out_shape=...  45.7 us
    unnamed x10, local copies, waits for them, and re-layouts  4.5 us

profile of v5, /device:TPU:1, one launch (start us, length us, event | category | flops | bytes accessed | tf_op | source)
XLA Modules:
  0.0 50.8 jit_solution(16878479010373408879)
XLA Ops:
  0.6 45.7 %shard_map.75 = (bf16[128,1024]{1,0:T(8,128)(2,1)}, bf16[128,1024]{1,0:T(8,128)(2,1)}, bf16[128,1024]{1,0:T(8,128)(2,1)}, bf16[128,1024]{1,0:T(8,128)(2,1)}) custom-call(bf16[128,1024]{1,0:T(8,128)(2,1)} %bitcast.12, bf16[128,1024]{1,0:T(8,128)(2,1)} %bitcast.13, bf16[128,1024]{1,0:T(8,128)(2,1)} %bitcast.14, bf16[128,1024]{1,0:T(8,128)(2,1)} %bitcast.15), custom_call_target="tpu_custom_call" | custom-call | tf_op jit(solution)/shard_map/pallas_call | solution.py:442
  46.3 0.0 copy-start.2
  46.3 1.7 %copy.12 = bf16[16,8,1024]{2,1,0:T(8,128)(2,1)} copy(bf16[16,8,1024]{2,1,0:T(8,128)(2,1)} %bitcast.11) | data formatting | bytes 524288
  48.0 0.0 copy-done.2
  48.0 0.0 copy-start.1
  48.0 0.7 %copy.13 = bf16[16,8,1024]{2,1,0:T(8,128)(2,1)} copy(bf16[16,8,1024]{2,1,0:T(8,128)(2,1)S(1)} %bitcast.10) | data formatting | bytes 524288
  48.7 0.3 copy-done.1
  49.1 0.0 copy-start
  49.1 0.7 %copy.14 = bf16[16,8,1024]{2,1,0:T(8,128)(2,1)} copy(bf16[16,8,1024]{2,1,0:T(8,128)(2,1)S(1)} %bitcast.9) | data formatting | bytes 524288
  49.8 0.3 copy-done
  50.1 0.7 %copy.15 = bf16[16,8,1024]{2,1,0:T(8,128)(2,1)} copy(bf16[16,8,1024]{2,1,0:T(8,128)(2,1)S(1)} %bitcast.8) | data formatting | bytes 524288
Async XLA Ops:
  46.3 1.7 %copy-start.2 = (bf16[128,1024]{1,0:T(8,128)(2,1)S(1)}, bf16[128,1024]{1,0:T(8,128)(2,1)}, u32[]{:S(2)}) copy-start(bf16[128,1024]{1,0:T(8,128)(2,1)} %get-tuple-element.9) | copy-start | bytes 786436
  48.0 1.0 %copy-start.1 = (bf16[128,1024]{1,0:T(8,128)(2,1)S(1)}, bf16[128,1024]{1,0:T(8,128)(2,1)}, u32[]{:S(2)}) copy-start(bf16[128,1024]{1,0:T(8,128)(2,1)} %get-tuple-element.10) | copy-start | bytes 786436
  49.1 1.0 %copy-start = (bf16[128,1024]{1,0:T(8,128)(2,1)S(1)}, bf16[128,1024]{1,0:T(8,128)(2,1)}, u32[]{:S(2)}) copy-start(bf16[128,1024]{1,0:T(8,128)(2,1)} %get-tuple-element.11) | copy-start | bytes 786436

commit v6 on v5

--- a/solution.py
+++ b/solution.py
@@ -75,9 +75,9 @@
     return jnp.dot(a, b, preferred_element_type=F32)
 
 
-def kernel(n_lat, n_lon, pairs, q_hbm, k_hbm, v_hbm, c_hbm, o_hbm, dq_hbm, dk_hbm, dv_hbm,
-           inputs, outputs, ext, snd_side, snd_corner, relay, bias1, bias2, perm, stat_acc, stat_own, stat_in,
-           stat_ext, in_sem, out_sem, side_s, side_r, corner_s, corner_r, cut_s, strip_s, strip_r, relay_r, pass_s,
+def kernel(n_lat, n_lon, pairs, q_hbm, k_hbm, v_hbm, c_hbm, outputs,
+           inputs, ext, snd_side, snd_corner, relay, bias1, bias2, perm, stat_acc, stat_own, stat_in,
+           stat_ext, in_sem, side_s, side_r, corner_s, corner_r, cut_s, strip_s, strip_r, relay_r, pass_s,
            stat_s, stat_r):
     lat, lon = lax.axis_index("lat"), lax.axis_index("lon")
     x = lax.rem(lat, XS)
@@ -97,8 +97,6 @@
 
     loads = [pltpu.make_async_copy(ref, inputs.at[i], in_sem.at[i])
              for i, ref in enumerate((k_hbm, v_hbm, q_hbm, c_hbm))]
-    stores = [pltpu.make_async_copy(outputs.at[i], ref, out_sem.at[i])
-              for i, ref in enumerate((o_hbm, dq_hbm, dk_hbm, dv_hbm))]
     for load in loads:
         load.start()
 
@@ -406,16 +404,12 @@
     wait_corners(1)
     lax.fori_loop(half, pairs, forward, 0, unroll=4)
     send_stats(1)
-    stores[0].start()
-    stores[1].start()
     spread_stats(0)
     wait_corners(2)
     lax.fori_loop(0, half, backward, 0, unroll=4)
     spread_stats(1)
     wait_corners(3)
     lax.fori_loop(half, pairs, backward, 0, unroll=4)
-    stores[2].start()
-    stores[3].start()
 
     for c in range(4):
         sent_strips(c)
@@ -426,6 +420,13 @@
     for i in range(2):
         for copy in stats(i):
             copy.wait_send()
+
+
+def handed_out(outputs, o_hbm, dq_hbm, dk_hbm, dv_hbm, sem):
+    stores = [pltpu.make_async_copy(outputs.at[i], ref, sem.at[i])
+              for i, ref in enumerate((o_hbm, dq_hbm, dk_hbm, dv_hbm))]
+    for store in stores:
+        store.start()
     for store in stores:
         store.wait()
 
@@ -438,14 +439,14 @@
         pairs = width // 128
         heads = 2 * pairs
         flat = [x.reshape(OWN, width) for x in (queries, keys, values, cotangent)]
+        flat = [pltpu.with_memory_space_constraint(x, pltpu.HBM) for x in flat]
         dma = pltpu.SemaphoreType.DMA
         outs = pl.pallas_call(
             functools.partial(kernel, n_lat, n_lon, pairs),
-            out_shape=[jax.ShapeDtypeStruct((OWN, width), BF16)] * 4,
+            out_shape=jax.ShapeDtypeStruct((4, OWN, width), BF16),
             in_specs=[pl.BlockSpec(memory_space=pltpu.HBM)] * 4,
-            out_specs=[pl.BlockSpec(memory_space=pltpu.HBM)] * 4,
+            out_specs=pl.BlockSpec(memory_space=pltpu.VMEM),
             scratch_shapes=[
-                pltpu.VMEM((4, OWN, width), BF16),
                 pltpu.VMEM((4, OWN, width), BF16),
                 pltpu.VMEM((4, pairs, EXT, 128), BF16),
                 pltpu.VMEM((2, 4, pairs, 96, 128), BF16),
@@ -458,12 +459,19 @@
                 pltpu.VMEM((2, heads, OWN), F32),
                 pltpu.VMEM((2, 8, heads, OWN), F32),
                 pltpu.VMEM((2 * heads, 1, EXT), F32),
-                dma((4,)), dma((4,)), dma((4, 2)), dma((4, 2)), dma((4, 2, 2)), dma((4, 2, 2)), dma((4, 2, 2)),
+                dma((4,)), dma((4, 2)), dma((4, 2)), dma((4, 2, 2)), dma((4, 2, 2)), dma((4, 2, 2)),
                 dma((4, 2, XS)), dma((4, 2, XS)), dma((4, 2)), dma((4, 2)), dma((2, 8)), dma((2, 8)),
             ],
             compiler_params=pltpu.CompilerParams(
-                collective_id=0, has_side_effects=True, vmem_limit_bytes=63 * 1024 * 1024),
+                collective_id=0, has_side_effects=True, vmem_limit_bytes=48 * 1024 * 1024),
         )(*flat)
+        outs = pl.pallas_call(
+            handed_out,
+            out_shape=[jax.ShapeDtypeStruct((OWN, width), BF16)] * 4,
+            in_specs=[pl.BlockSpec(memory_space=pltpu.VMEM)],
+            out_specs=[pl.BlockSpec(memory_space=pltpu.HBM)] * 4,
+            scratch_shapes=[dma((4,))],
+        )(outs)
         return tuple(x.reshape(ROWS, COLS, width) for x in outs)
 
     spec = P("lat", "lon", None)

time: 51 us -> 49 us (0.961)
  local copies, waits for them, and re-layouts: 4.5 us -> 0.97 us
  Pallas kernels: 45.7 us -> 47.2 us
    unnamed x10 -> x2, local copies, waits for them, and re-layouts: 4.5 us -> 0.97 us
    pallas_call x0 -> x1, Pallas kernels: none -> 2.22 us  [shards(): pl.pallas_call(handed_out, out_shape=[jax.ShapeDtypeStruct((OWN, width),...]
    pallas_call x1, Pallas kernels: 45.7 us -> 45 us  [shards(): pl.pallas_call(functools.partial(kernel, n_lat, n_lon, pairs), out_shape=...]
where the time goes in v6:
time: 49 us; the launch traced here: 48.9 us
  Pallas kernels  47.2 us (96%)
  local copies, waits for them, and re-layouts  0.97 us (2%)
  between operations  0.65 us (1%)
    pallas_call x1, Pallas kernels, shards(): pl.pallas_call(functools.partial(kernel, n_lat, n_lon, pairs), out_shape=...  45 us
    pallas_call x1, Pallas kernels, shards(): pl.pallas_call(handed_out, out_shape=[jax.ShapeDtypeStruct((OWN, width),...  2.22 us

profile of v6, /device:TPU:1, one launch (start us, length us, event | category | flops | bytes accessed | tf_op | source)
XLA Modules:
  0.0 48.9 jit_solution(3820092430223670137)
XLA Ops:
  0.6 45.0 %shard_map.75.outputs = bf16[4,128,1024]{2,1,0:T(8,128)(2,1)S(1)} custom-call(bf16[128,1024]{1,0:T(8,128)(2,1)} %bitcast.8, bf16[128,1024]{1,0:T(8,128)(2,1)} %bitcast.9, bf16[128,1024]{1,0:T(8,128)(2,1)} %bitcast.10, bf16[128,1024]{1,0:T(8,128)(2,1)} %bitcast.11), custom_call_target="tpu_custom_call" | custom-call | tf_op jit(solution)/shard_map/pallas_call | solution.py:444
  45.7 0.0 copy-start
  45.7 1.0 %copy-done = bf16[4,128,1024]{2,1,0:T(8,128)(2,1)} copy-done((bf16[4,128,1024]{2,1,0:T(8,128)(2,1)}, bf16[4,128,1024]{2,1,0:T(8,128)(2,1)S(1)}, u32[]{:S(2)}) %copy-start) | copy-done | bytes 1048600
  46.6 2.2 %shard_map.76 = (bf16[128,1024]{1,0:T(8,128)(2,1)}, bf16[128,1024]{1,0:T(8,128)(2,1)}, bf16[128,1024]{1,0:T(8,128)(2,1)}, bf16[128,1024]{1,0:T(8,128)(2,1)}) custom-call(bf16[4,128,1024]{2,1,0:T(8,128)(2,1)} %copy-done), custom_call_target="tpu_custom_call" | custom-call | tf_op jit(solution)/shard_map/pallas_call | solution.py:468
Async XLA Ops:
  45.7 1.0 %copy-start = (bf16[4,128,1024]{2,1,0:T(8,128)(2,1)}, bf16[4,128,1024]{2,1,0:T(8,128)(2,1)S(1)}, u32[]{:S(2)}) copy-start(bf16[4,128,1024]{2,1,0:T(8,128)(2,1)S(1)} %shard_map.75.outputs) | copy-start | bytes 3145732
